TPU v7x, 128 devices: a whole 4x4x4 slice. The times are simulated.
128 devices in a mesh: curve: 32 (over y, z, core), sub: 4 (over x).
Axes of the slice: x: 4, y: 4, z: 4, core: 2. Of those that a mesh axis runs over, the one named last changes fastest.
Arguments:
- prognostic: float32 [4, 768, 32, 4, 4, 128], P(None, 'curve', 'sub'), may hold values from -6 to 6
- layer_mass: float32 [768, 32, 4, 4, 128], P('curve', 'sub'), may hold values from 0.5 to 2
- column_aux: bfloat16 [196608, 1013], P(('curve', 'sub')), may hold values from -6 to 6
- group_owner: int32 [98304, 1], P(('curve', 'sub')), may hold values from 0 to 127; in each aligned block of 768 rows (0 to 767, 768 to 1535, ...) at most 12 rows name the same one
- weight_in: bfloat16 [1525, 2048], replicated, may hold values from -0.15625 to 0.15625
- bias_in: float32 [2048], replicated, may hold values from -3 to 3
- weight_out: bfloat16 [2048, 512], replicated, may hold values from -0.125 to 0.125
- bias_out: float32 [512], replicated, may hold values from -2 to 2
Outputs:
- advanced: float32 [4, 768, 32, 4, 4, 128], P(None, 'curve', 'sub')
Inputs may be any that keep to these rules, and one draw needn't show every extreme that they name: `group_owner`: among the 768 columns of one device, at most 12 name the same owner, and every device owns some column.
All inputs are finite; a program needn't handle non-finite values.
Results may differ from a plain program's by a relative error of at most 0.0035.
Values may be sent and summed in bfloat16 or wider, within the bound.
A program may use at most 128 MiB of HBM per device.

v0:
```python
import jax
import jax.numpy as jnp
import numpy as np
from jax import lax
from jax.sharding import PartitionSpec as P

section_step = 0.1


def with_halo(cells, sides, width):
    for axis, dim in sides:
        count = lax.axis_size(axis)
        head = lax.slice_in_dim(cells, 0, width, axis=dim)
        tail = lax.slice_in_dim(cells, cells.shape[dim] - width, cells.shape[dim], axis=dim)
        cells = jnp.concatenate(
            [
                lax.ppermute(tail, axis, [(i, (i + 1) % count) for i in range(count)]),
                cells,
                lax.ppermute(head, axis, [((i + 1) % count, i) for i in range(count)]),
            ],
            axis=dim,
        )
    return cells


def node_tables():
    nodes = np.array([-1.0, -1.0 / np.sqrt(5.0), 1.0 / np.sqrt(5.0), 1.0])
    quadrature = np.array([1.0 / 6.0, 5.0 / 6.0, 5.0 / 6.0, 1.0 / 6.0])
    products = np.array(
        [
            np.prod(
                [
                    nodes[left_node] - nodes[other_node]
                    for other_node in range(4)
                    if other_node != left_node
                ]
            )
            for left_node in range(4)
        ]
    )
    derivative = np.zeros((4, 4))
    for left_node in range(4):
        for other_node in range(4):
            if left_node != other_node:
                derivative[left_node, other_node] = products[left_node] / (
                    products[other_node] * (nodes[left_node] - nodes[other_node])
                )
            else:
                derivative[left_node, left_node] = sum(
                    (
                        1.0 / (nodes[left_node] - nodes[third_node])
                        for third_node in range(4)
                        if third_node != left_node
                    )
                )
    return (derivative.astype(np.float32), quadrature.astype(np.float32))


def advect(prognostic, derivative):
    along_first = jnp.einsum(
        "ik,fabkjl->fabijl", derivative, prognostic, precision=lax.Precision.HIGHEST
    )
    along_second = jnp.einsum(
        "jk,fabikl->fabijl", derivative, prognostic, precision=lax.Precision.HIGHEST
    )
    return -(prognostic[0:1] * along_first + prognostic[1:2] * along_second)


def node_mass(layer_mass, quadrature):
    return quadrature[:, None, None] * quadrature[None, :, None] * layer_mass


def cell_average(prognostic, node_weight):
    fields = prognostic.shape[0]
    rows_a, rows_b, levels = (node_weight.shape[0], node_weight.shape[1], node_weight.shape[4])
    weighted = (prognostic * node_weight[None]).reshape(fields, rows_a, rows_b, 2, 2, 2, 2, levels)
    weighted_sum = jnp.sum(weighted, axis=(4, 6))
    mass_sum = jnp.sum(node_weight.reshape(rows_a, rows_b, 2, 2, 2, 2, levels), axis=(3, 5))
    return weighted_sum / mass_sum[None]


def spread_cells(cells):
    return jnp.repeat(jnp.repeat(cells, 2, axis=3), 2, axis=4)


def apply_network(inputs, weight_in, bias_in, weight_out, bias_out):
    hidden = jax.nn.silu(
        jnp.dot(inputs, weight_in, preferred_element_type=jnp.float32) + bias_in
    ).astype(jnp.bfloat16)
    return (jnp.dot(hidden, weight_out, preferred_element_type=jnp.float32) + bias_out).astype(
        jnp.bfloat16
    )


def relay(buffer):
    return lax.all_to_all(buffer, ("curve", "sub"), split_axis=0, concat_axis=0, tiled=True)


def shards(
    prognostic, layer_mass, column_aux, group_owner, weight_in, bias_in, weight_out, bias_out
):
    derivative_np, quadrature_np = node_tables()
    derivative = jnp.asarray(derivative_np)
    quadrature = jnp.asarray(quadrature_np)
    fields = prognostic.shape[0]
    rows_a, rows_b, levels = (prognostic.shape[1], prognostic.shape[2], prognostic.shape[5])
    advection = advect(prognostic, derivative)
    node_weight = node_mass(layer_mass, quadrature)
    stacked = jnp.concatenate([advection * node_weight[None], node_weight[None]], axis=0)
    rims = jnp.stack([stacked[:, :, :, 0], stacked[:, :, :, 3]], axis=3)
    padded = with_halo(rims.astype(jnp.bfloat16), (("curve", 1),), 1).astype(rims.dtype)
    passed = jnp.concatenate(
        [
            (stacked[:, :, :, 0] + padded[:, :-2, :, 1])[:, :, :, None],
            stacked[:, :, :, 1:3],
            (stacked[:, :, :, 3] + padded[:, 2:, :, 0])[:, :, :, None],
        ],
        axis=3,
    )
    rims = jnp.stack([passed[:, :, :, :, 0], passed[:, :, :, :, 3]], axis=4)
    padded = with_halo(rims.astype(jnp.bfloat16), (("sub", 2),), 1).astype(rims.dtype)
    summed = jnp.concatenate(
        [
            (passed[:, :, :, :, 0] + padded[:, :, :-2, :, 1])[:, :, :, :, None],
            passed[:, :, :, :, 1:3],
            (passed[:, :, :, :, 3] + padded[:, :, 2:, :, 0])[:, :, :, :, None],
        ],
        axis=4,
    )
    section = prognostic + section_step * (summed[:fields] / summed[fields:])
    cells = cell_average(prognostic, node_weight)
    col_count = group_owner.shape[0]
    state_cols = (
        cells.transpose(1, 2, 3, 4, 0, 5).reshape(col_count, fields * levels).astype(jnp.bfloat16)
    )
    devices = lax.axis_size("curve") * lax.axis_size("sub")
    capacity = column_aux.shape[0] // devices
    targets = group_owner[:, 0]
    hits = (targets[:, None] == jnp.arange(devices, dtype=jnp.int32)[None]).astype(jnp.float32)
    positions = jnp.arange(col_count, dtype=jnp.int32)
    before = (positions[:, None] > positions[None, :]).astype(jnp.float32)
    earlier = jnp.dot(before, hits, precision=lax.Precision.HIGHEST)
    slot_index = jnp.sum(hits * earlier, axis=1).astype(jnp.int32)
    position = targets * capacity + slot_index
    selector = (position[:, None] == jnp.arange(devices * capacity, dtype=jnp.int32)[None]).astype(
        jnp.bfloat16
    )
    aux_width = column_aux.shape[1]
    aux_home = relay(column_aux.reshape(devices, capacity, aux_width)).reshape(
        devices * capacity, aux_width
    )
    aux_cols = jnp.dot(selector, aux_home, preferred_element_type=jnp.float32).astype(jnp.bfloat16)
    col_increment = apply_network(
        jnp.concatenate([state_cols, aux_cols], axis=1), weight_in, bias_in, weight_out, bias_out
    )
    back = col_increment.reshape(rows_a, rows_b, 2, 2, fields, levels).transpose(4, 0, 1, 2, 3, 5)
    return section + spread_cells(back.astype(jnp.float32))


def solution(mesh):
    return jax.shard_map(
        shards,
        mesh=mesh,
        in_specs=(
            P(None, "curve", "sub", None, None, None),
            P("curve", "sub", None, None, None),
            P(("curve", "sub"), None),
            P(("curve", "sub"), None),
            P(),
            P(),
            P(),
            P(),
        ),
        out_specs=P(None, "curve", "sub", None, None, None),
        check_vma=False,
    )
```

profile of v0, /device:TPU:0, one launch (start us, length us, event | category | flops | bytes accessed | tf_op | source)
XLA Modules:
  0.0 199.8 jit_solution(11956521490568149251)
XLA Ops:
  0.0 0.9 broadcast_multiply_fusion
  0.9 3.3 %copy_multiply_fusion.1 = f32[24,8,4,4,128]{4,2,3,1,0:T(4,128)} fusion(f32[24,8,4,4,128]{4,3,2,1,0:T(4,128)} %param.11, f32[4,4]{0,1:T(4,128)S(1)} %broadcast_multiply_fusion), kind=kLoop, calls=%fused_computation.42 | loop fusion | flops 393216 | bytes 3145792 | tf_op jit(solution)/shard_map/mul | solution.py:70
  4.2 3.1 %fusion.47 = f32[1,24,8,4,4,128]{5,3,4,2,1,0:T(4,128)} fusion(f32[24,8,4,4,128]{4,3,2,1,0:T(4,128)} %param.11, f32[4,4]{0,1:T(4,128)S(1)} %broadcast_multiply_fusion), kind=kLoop, calls=%fused_computation.70 | loop fusion | flops 393216 | bytes 3145792 | tf_op jit(solution)/shard_map/broadcast_in_dim | solution.py:109
  7.3 0.9 slice_bitcast_fusion.1
  8.2 1.6 copy.30
  9.9 1.7 copy.32
  11.6 13.2 %fusion.40 = f32[4,4,24,8,4,128]{5,0,4,3,2,1:T(4,128)} fusion(f32[4,4,1,1,1,1]{1,0,5,4,3,2:T(4,128)S(1)} %copy-done.9, f32[4,24,8,4,4,128]{5,4,3,2,1,0:T(4,128)S(1)} %copy-done.1), kind=kOutput, calls=%fused_computation.69 | convolution fusion | flops 75497472 | bytes 12582976 | tf_op jit(solution)/shard_map/jk,fabikl->fabijl/dot_general | solution.py:63
  24.8 17.5 %fusion.8 = f32[4,24,8,4,4,128]{5,3,4,2,1,0:T(4,128)S(1)} fusion(f32[4,4,24,8,4,128]{5,0,4,3,2,1:T(4,128)} %fusion.40, f32[24,8,4,4,128]{4,2,3,1,0:T(4,128)} %copy_multiply_fusion.1, f32[24,8,4,4,128]{4,2,3,1,0:T(4,128)} %copy.32, f32[24,8,4,4,128]{4,2,3,1,0:T(4,128)} %copy.30, f32[4,4,1,1,1,1]{1,0,5,4,3,2:T(4,128)S(1)} %copy-done.9, ...), kind=kOutput, calls=%fused_computation.14 | convolution fusion | flops 83361792 | bytes 23593024 | tf_op jit(solution)/shard_map/ik,fabkjl->fabijl/dot_general | solution.py:60
  42.3 8.0 %fusion.37 = (bf16[5,24,8,1,4,128]{5,3,4,2,1,0:T(2,128)(2,1)S(1)}, f32[5,24,8,1,4,128]{5,3,4,2,1,0:T(1,128)}, bf16[5,24,8,1,4,128]{5,3,4,2,1,0:T(2,128)(2,1)S(1)}, f32[5,24,8,1,4,128]{5,3,4,2,1,0:T(1,128)}) fusion(f32[1,24,8,4,4,128]{5,3,4,2,1,0:T(4,128)} %fusion.47, f32[4,24,8,4,4,128]{5,3,4,2,1,0:T(4,128)S(1)} %fusion.8), kind=kLoop, calls=%fused_computation.66 | loop fusion | flops 1966080 | bytes 13762560 | tf_op jit(solution)/shard_map/convert.4
  50.4 1.3 copy-done.3
  51.7 0.4 pad_maximum_fusion.12
  52.0 0.3 copy-done.4
  52.3 6.0 %collective-permute-start.1 = (bf16[5,1,8,2,4,128]{5,3,4,2,1,0:T(2,128)(2,1)S(1)}, bf16[5,1,8,2,4,128]{5,3,4,2,1,0:T(2,128)(2,1)S(1)}, u32[]{:S(2)}, u32[]{:S(2)}) collective-permute-start(bf16[5,1,8,2,4,128]{5,3,4,2,1,0:T(2,128)(2,1)S(1)} %get-tuple-element.20), channel_id=1, source_target_pairs={{4,0},{8,4},{12,8},{16,12},{20,16},{24,20},{28,24},{32,28},{36,32}... | collective-permute-start | bytes 245768 | tf_op jit(solution)/shard_map/ppermute | solution.py:19
  58.3 4.6 %copy.38 = bf16[1536,1013]{1,0:T(8,128)(2,1)} copy(bf16[1536,1013]{0,1:T(8,128)(2,1)} %param.12) | data formatting | bytes 6223872 | tf_op args[2]
  63.0 6.6 %reshape.75 = bf16[128,12,1013]{2,1,0:T(8,128)(2,1)} reshape(bf16[1536,1013]{1,0:T(8,128)(2,1)} %copy.38) | data formatting | bytes 6223872 | tf_op jit(solution)/shard_map/reshape | solution.py:149
  69.5 7.6 %all-to-all-start = ((bf16[128,12,1013]{2,1,0:T(8,128)(2,1)}), bf16[128,12,1013]{2,1,0:T(8,128)(2,1)}, u32[]{:S(2)}, u32[]{:S(2)}) async-start(bf16[128,12,1013]{2,1,0:T(8,128)(2,1)} %reshape.75), calls=%async_computation | async-start | bytes 8388608 | tf_op jit(solution)/shard_map/all_to_all | solution.py:96
  77.1 9.2 %copy_multiply_fusion = f32[4,24,8,4,4,128]{5,3,4,2,1,0:T(4,128)} fusion(f32[4,24,8,4,4,128]{5,4,3,2,1,0:T(4,128)} %param.10, f32[24,8,4,4,128]{4,2,3,1,0:T(4,128)} %copy_multiply_fusion.1), kind=kLoop, calls=%fused_computation.17 | loop fusion | flops 1572864 | bytes 14155776 | tf_op jit(solution)/shard_map/mul | solution.py:76
  86.3 11.0 %reduce_sum.27 = f32[4,24,8,2,2,128]{5,3,4,2,1,0:T(2,128)} reduce(f32[4,24,8,2,2,2,2,128]{7,4,3,6,5,2,1,0:T(2,128)} %bitcast.45, f32[]{:T(128)} %constant.5.clone.1), dimensions={4,6}, to_apply=%region_0.0 | reduce | flops 1179648 | bytes 7864324 | tf_op jit(solution)/shard_map/reduce_sum | solution.py:77
  97.2 3.0 %reduce_sum.28 = f32[24,8,2,2,128]{4,2,3,1,0:T(2,128)S(1)} reduce(f32[24,8,2,2,2,2,128]{6,3,2,5,4,1,0:T(2,128)} %bitcast.46, f32[]{:T(128)} %constant.5.clone.1), dimensions={3,5}, to_apply=%region_1.0 | reduce | flops 294912 | bytes 1966084 | tf_op jit(solution)/shard_map/reduce_sum | solution.py:78
  100.2 2.3 %fusion.32 = bf16[24,8,2,2,4,128]{5,2,3,1,0,4:T(2,128)(2,1)S(1)} fusion(f32[4,24,8,2,2,128]{5,3,4,2,1,0:T(2,128)} %reduce_sum.27, f32[24,8,2,2,128]{4,2,3,1,0:T(2,128)S(1)} %reduce_sum.28), kind=kLoop, calls=%fused_computation.55 | loop fusion | flops 786432 | bytes 2752512 | tf_op jit(solution)/shard_map/convert_element_type | solution.py:134
  102.5 1.4 copy.37
  103.9 0.1 copy.55
  104.1 1.2 copy.39
  105.3 20.6 %convert_add_fusion.1 = (f32[5,24,8,1,4,128]{5,3,4,2,1,0:T(1,128)S(1)}, f32[5,24,8,1,4,128]{5,3,4,2,1,0:T(1,128)S(1)}) fusion(f32[5,24,8,1,4,128]{5,3,4,2,1,0:T(1,128)} %get-tuple-element.6, bf16[5,1,8,2,4,128]{5,3,4,2,1,0:T(2,128)(2,1)S(1)} %collective-permute-done.1, bf16[5,1,8,2,4,128]{5,3,4,2,1,0:T(2,128)(2,1)S(1)} %collective-permute-done, ...), kind=kLoop, calls=%fused_computation.34 | loop fusion | flops 8847360 | bytes 9994240 | tf_op jit(solution)/shard_map/add | solution.py:114
  126.0 5.7 %fusion.1 = f32[5,24,8,4,4,128]{5,3,4,2,1,0:T(4,128)S(1)} fusion(f32[1,24,8,4,4,128]{5,3,4,2,1,0:T(4,128)S(1)} %copy-done.5, f32[4,24,8,4,4,128]{5,3,4,2,1,0:T(4,128)S(1)} %bitcast.44, f32[5,24,8,1,4,128]{5,3,4,2,1,0:T(1,128)S(1)} %get-tuple-element.18, f32[5,24,8,1,4,128]{5,3,4,2,1,0:T(1,128)S(1)} %get-tuple-element.17), kind=kLoop, calls=%fused_computation.4 | loop fusion | flops 15728640 | bytes 19660800 | tf_op jit(solution)/shard_map/concatenate | solution.py:112
  131.7 0.9 fusion.39
  132.6 0.4 pad_maximum_fusion.10
  133.0 1.0 collective-permute-start.2
  133.9 2.4 %collective-permute-start.3 = (bf16[5,24,1,4,2,128]{5,3,4,2,1,0:T(4,128)(2,1)S(1)}, bf16[5,24,1,4,2,128]{5,3,4,2,1,0:T(4,128)(2,1)S(1)}, u32[]{:S(2)}, u32[]{:S(2)}) collective-permute-start(bf16[5,24,1,4,2,128]{5,3,4,2,1,0:T(4,128)(2,1)S(1)} %get-tuple-element.22), channel_id=1, source_target_pairs={{1,0},{2,1},{3,2},{0,3},{5,4},{6,5},{7,6},{4,7},{9,8},{10,9},{11,1... | collective-permute-start | bytes 737288 | tf_op jit(solution)/shard_map/ppermute | solution.py:19
  136.3 0.4 fusion.31
  136.7 0.8 slice.78
  137.5 4.0 %collective-permute-done.2 = bf16[5,24,1,4,2,128]{5,3,4,2,1,0:T(4,128)(2,1)S(1)} collective-permute-done((bf16[5,24,1,4,2,128]{5,3,4,2,1,0:T(4,128)(2,1)S(1)}, bf16[5,24,1,4,2,128]{5,3,4,2,1,0:T(4,128)(2,1)S(1)}, u32[]{:S(2)}, u32[]{:S(2)}) %collective-permute-start.2) | collective-permute-done | bytes 245792 | tf_op jit(solution)/shard_map/ppermute | solution.py:17
  141.5 0.2 collective-permute-done.3
  141.6 1.9 convert_add_fusion
  143.6 1.6 maximum_bitcast_fusion
  145.1 4.2 %pad_maximum_fusion = f32[5,24,8,4,4,128]{5,3,4,2,1,0:T(4,128)} fusion(f32[5,24,8,4,1,128]{5,3,4,2,1,0:T(4,128)S(1)} %get-tuple-element.10, f32[5,24,8,4,2,128]{5,3,4,2,1,0:T(4,128)S(1)} %slice.78, f32[5,24,8,4,1,128]{5,3,4,2,1,0:T(4,128)S(1)} %get-tuple-element.9), kind=kLoop, calls=%fused_computation.5 | loop fusion | flops 3932160 | bytes 15728640 | tf_op jit(solution)/shard_map/concatenate | solution.py:122
  149.3 6.6 %reshape.76 = bf16[1536,1013]{1,0:T(8,128)(2,1)} reshape(bf16[128,12,1013]{2,1,0:T(8,128)(2,1)} %all-to-all-done) | data formatting | bytes 6223872 | tf_op jit(solution)/shard_map/reshape | solution.py:149
  156.0 6.1 %fusion.21 = bf16[768,1013]{0,1:T(8,128)(2,1)} fusion(bf16[1536,1013]{1,0:T(8,128)(2,1)} %reshape.76, s32[768]{0:T(1024)S(1)} %add_reduce_fusion), kind=kOutput, calls=%fused_computation.40 | convolution fusion | flops 2391924480 | bytes 4670976 | tf_op jit(solution)/shard_map/dot_general | solution.py:152
  162.1 11.8 %fusion.27 = f32[768,512]{1,0:T(8,128)} fusion(bf16[2048,512]{1,0:T(8,128)(2,1)S(1)} %copy-done, bf16[1525,2048]{1,0:T(8,128)(2,1)} %param.14, f32[2048]{0:T(1024)S(1)} %copy-done.10, bf16[768,1013]{0,1:T(8,128)(2,1)} %fusion.21, bf16[768,512]{0,1:T(8,128)(2,1)S(1)} %copy-done.7, f32[512]{0:T(512)S(1)} %copy-done.11), kind=kOutput, calls=%fused_computation.48 | convolution fusion | flops 6423149568 | bytes 12269056 | tf_op jit(solution)/shard_map/dot_general | solution.py:90
  173.9 3.0 %reshape.79 = f32[24,8,2,2,4,128]{5,4,3,2,1,0:T(4,128)} reshape(f32[768,512]{1,0:T(8,128)} %fusion.27) | data formatting | bytes 3145728 | tf_op jit(solution)/shard_map/convert_element_type | solution.py:157
  176.9 2.2 %copy.40 = f32[4,24,8,2,2,128]{5,3,4,2,1,0:T(2,128)S(1)} copy(f32[4,24,8,2,2,128]{5,0,4,3,2,1:T(4,128)} %bitcast.49) | data formatting | bytes 3145728 | tf_op jit(solution)/shard_map/convert_element_type | solution.py:157
  179.2 1.1 broadcast_in_dim.7
  180.3 0.0 slice-start.1
  180.3 1.0 broadcast_in_dim.8
  181.4 0.9 slice-done.1
  182.2 0.4 copy-done.6
  182.7 8.4 %fusion.5 = f32[4,24,8,4,4,128]{5,3,4,2,1,0:T(4,128)} fusion(f32[4,24,8,4,4,128]{5,3,4,2,1,0:T(4,128)S(1)} %bitcast.47, f32[5,24,8,4,4,128]{5,3,4,2,1,0:T(4,128)} %pad_maximum_fusion, f32[4,24,8,4,4,128]{5,4,3,2,1,0:T(4,128)S(1)} %bitcast.42, f32[24,8,4,4,128]{4,2,3,1,0:T(4,128)S(1)} %copy-done.6), kind=kLoop, calls=%fused_computation.10 | loop fusion | flops 6291456 | bytes 26738688 | tf_op jit(solution)/shard_map/add | solution.py:157
  191.0 8.5 %copy.41 = f32[4,24,8,4,4,128]{5,4,3,2,1,0:T(4,128)} copy(f32[4,24,8,4,4,128]{5,3,4,2,1,0:T(4,128)} %fusion.5) | data formatting | bytes 12582912 | tf_op jit(solution)/shard_map/add | solution.py:157
  (36 shorter events, 0.1 us)
Async XLA Ops:
  0.0 162.1 %copy-start = (bf16[2048,512]{1,0:T(8,128)(2,1)S(1)}, bf16[2048,512]{1,0:T(8,128)(2,1)}, u32[]{:S(2)}) copy-start(bf16[2048,512]{1,0:T(8,128)(2,1)} %param.16) | copy-start | bytes 6291460
  0.9 6.4 %copy-start.1 = (f32[4,24,8,4,4,128]{5,4,3,2,1,0:T(4,128)S(1)}, f32[4,24,8,4,4,128]{5,4,3,2,1,0:T(4,128)}, u32[]{:S(2)}) copy-start(f32[4,24,8,4,4,128]{5,4,3,2,1,0:T(4,128)} %param.10) | copy-start | bytes 18874372
  9.9 1.7 copy-start.9
  42.3 8.1 %copy-start.2 = (f32[4,24,8,4,4,128]{5,3,4,2,1,0:T(4,128)}, f32[4,24,8,4,4,128]{5,3,4,2,1,0:T(4,128)S(1)}, u32[]{:S(2)}) copy-start(f32[4,24,8,4,4,128]{5,3,4,2,1,0:T(4,128)S(1)} %fusion.8) | copy-start | bytes 18874372
  50.4 1.3 copy-start.3
  50.4 1.9 copy-start.4
  52.3 53.0 %collective-permute-start = (bf16[5,1,8,2,4,128]{5,3,4,2,1,0:T(2,128)(2,1)S(1)}, bf16[5,1,8,2,4,128]{5,3,4,2,1,0:T(2,128)(2,1)S(1)}, u32[]{:S(2)}, u32[]{:S(2)}) collective-permute-start(bf16[5,1,8,2,4,128]{5,3,4,2,1,0:T(2,128)(2,1)S(1)} %get-tuple-element.19), channel_id=1, source_target_pairs={{0,4},{4,8},{8,12},{12,16},{16,20},{20,24},{24,28},{28,32},{32,36}... | collective-permute-start | bytes 245768 | tf_op jit(solution)/shard_map/ppermute | solution.py:17
  52.3 53.0 %collective-permute-start.1 = (bf16[5,1,8,2,4,128]{5,3,4,2,1,0:T(2,128)(2,1)S(1)}, bf16[5,1,8,2,4,128]{5,3,4,2,1,0:T(2,128)(2,1)S(1)}, u32[]{:S(2)}, u32[]{:S(2)}) collective-permute-start(bf16[5,1,8,2,4,128]{5,3,4,2,1,0:T(2,128)(2,1)S(1)} %get-tuple-element.20), channel_id=1, source_target_pairs={{4,0},{8,4},{12,8},{16,12},{20,16},{24,20},{28,24},{32,28},{36,32}... | collective-permute-start | bytes 245768 | tf_op jit(solution)/shard_map/ppermute | solution.py:19
  69.5 79.8 %all-to-all-start = ((bf16[128,12,1013]{2,1,0:T(8,128)(2,1)}), bf16[128,12,1013]{2,1,0:T(8,128)(2,1)}, u32[]{:S(2)}, u32[]{:S(2)}) async-start(bf16[128,12,1013]{2,1,0:T(8,128)(2,1)} %reshape.75), calls=%async_computation | async-start | bytes 8388608 | tf_op jit(solution)/shard_map/all_to_all | solution.py:96
  102.5 2.8 %copy-start.8 = (s32[768,1]{0,1:T(1,128)S(1)}, s32[768,1]{0,1:T(1,128)}, u32[]{:S(2)}) copy-start(s32[768,1]{0,1:T(1,128)} %param.13) | copy-start | bytes 9220
  105.3 20.7 %slice-start.2 = ((s8[6291456]{0:T(1024)(128)(4,1)}), s8[4194304]{0:T(1024)(128)(4,1)S(1)}, s32[]{:S(2)}) async-start(s8[6291456]{0:T(1024)(128)(4,1)} %bitcast.43), calls=%async_computation.3 | async-start | bytes 8388608
  105.3 20.7 %slice-start.3 = ((s8[6291456]{0:T(1024)(128)(4,1)}), s8[2097152]{0:T(1024)(128)(4,1)S(1)}, s32[]{:S(2)}) async-start(s8[6291456]{0:T(1024)(128)(4,1)} %bitcast.43), calls=%async_computation.4 | async-start | bytes 4194304
  105.3 20.7 %copy-start.5 = (f32[1,24,8,4,4,128]{5,3,4,2,1,0:T(4,128)S(1)}, f32[1,24,8,4,4,128]{5,3,4,2,1,0:T(4,128)}, u32[]{:S(2)}) copy-start(f32[1,24,8,4,4,128]{5,3,4,2,1,0:T(4,128)} %fusion.47) | copy-start | bytes 4718596
  133.0 8.5 %collective-permute-start.2 = (bf16[5,24,1,4,2,128]{5,3,4,2,1,0:T(4,128)(2,1)S(1)}, bf16[5,24,1,4,2,128]{5,3,4,2,1,0:T(4,128)(2,1)S(1)}, u32[]{:S(2)}, u32[]{:S(2)}) collective-permute-start(bf16[5,24,1,4,2,128]{5,3,4,2,1,0:T(4,128)(2,1)S(1)} %get-tuple-element.21), channel_id=1, source_target_pairs={{0,1},{1,2},{2,3},{3,0},{4,5},{5,6},{6,7},{7,4},{8,9},{9,10},{10,1... | collective-permute-start | bytes 737288 | tf_op jit(solution)/shard_map/ppermute | solution.py:17
  133.9 7.7 %collective-permute-start.3 = (bf16[5,24,1,4,2,128]{5,3,4,2,1,0:T(4,128)(2,1)S(1)}, bf16[5,24,1,4,2,128]{5,3,4,2,1,0:T(4,128)(2,1)S(1)}, u32[]{:S(2)}, u32[]{:S(2)}) collective-permute-start(bf16[5,24,1,4,2,128]{5,3,4,2,1,0:T(4,128)(2,1)S(1)} %get-tuple-element.22), channel_id=1, source_target_pairs={{1,0},{2,1},{3,2},{0,3},{5,4},{6,5},{7,6},{4,7},{9,8},{10,9},{11,1... | collective-permute-start | bytes 737288 | tf_op jit(solution)/shard_map/ppermute | solution.py:19
  156.0 6.1 %copy-start.7 = (bf16[768,512]{0,1:T(8,128)(2,1)S(1)}, bf16[768,512]{0,1:T(8,128)(2,1)}, u32[]{:S(2)}) copy-start(bf16[768,512]{0,1:T(8,128)(2,1)} %copy.39) | copy-start | bytes 2359300
  156.0 6.1 %copy-start.10 = (f32[2048]{0:T(1024)S(1)}, f32[2048]{0:T(1024)}, u32[]{:S(2)}) copy-start(f32[2048]{0:T(1024)} %param.15) | copy-start | bytes 24580
  156.0 6.1 %copy-start.11 = (f32[512]{0:T(512)S(1)}, f32[512]{0:T(512)}, u32[]{:S(2)}) copy-start(f32[512]{0:T(512)} %param.17) | copy-start | bytes 6148
  179.1 2.2 %slice-start = ((s8[6291456]{0:T(1024)(128)(4,1)}), s8[4194304]{0:T(1024)(128)(4,1)S(1)}, s32[]{:S(2)}) async-start(s8[6291456]{0:T(1024)(128)(4,1)} %bitcast.41), calls=%async_computation.1 | async-start | bytes 8388608
  180.3 1.9 slice-start.1
  180.3 2.3 %copy-start.6 = (f32[24,8,4,4,128]{4,2,3,1,0:T(4,128)S(1)}, f32[24,8,4,4,128]{4,2,3,1,0:T(4,128)}, u32[]{:S(2)}) copy-start(f32[24,8,4,4,128]{4,2,3,1,0:T(4,128)} %maximum_bitcast_fusion) | copy-start | bytes 4718596
where the time goes:
time: 203 us; the launch traced here: 200 us
  other arithmetic  83.8 us (41%)
  matrix products  49.1 us (24%)
  local copies, waits for them, and re-layouts  45.3 us (22%)
  starting transfers between devices  16.9 us (8%)
  waiting for transfers between devices  4.18 us (2%)
    add x1, other arithmetic, shards(): stacked[:, :, :, 0] + padded[:, :-2, :, 1]  20.6 us
    dot_general x1, matrix products, advect(): jnp.einsum('ik,fabkjl->fabijl', derivative, prognostic, precision=lax.Pre...  17.5 us
    dot_general x1, matrix products, advect(): jnp.einsum('jk,fabikl->fabijl', derivative, prognostic, precision=lax.Pre...  13.2 us
    dot_general x1, matrix products, apply_network(): jnp.dot(hidden, weight_out, preferred_element_type=jnp.float32) + bias_out  11.8 us
    reduce_sum x1, other arithmetic, cell_average(): weighted_sum = jnp.sum(weighted, axis=(4, 6))  11 us
    mul x1, other arithmetic, cell_average(): prognostic * node_weight[None]  9.15 us
    add x1, local copies, waits for them, and re-layouts, shards(): return section + spread_cells(back.astype(jnp.float32))  8.52 us
    ppermute x2, starting transfers between devices, with_halo(): lax.ppermute(head, axis, [((i + 1) % count, i) for i in range(count)])  8.36 us
  transfers between devices with their start and end apart: 5, of which 2 were waited for; matrix products, arithmetic and copies ran while one was open for 38% of the time, Pallas kernels for 0%

commit v1 on v0

v1 whole, which is shorter than its diff:
```python
import jax
import jax.numpy as jnp
import numpy as np
from jax import lax
from jax.experimental import pallas as pl
from jax.experimental.pallas import tpu as pltpu
from jax.sharding import PartitionSpec as P

section_step = 0.1
NF, EA, EB, LEV = 4, 24, 8, 128
DEV, CAP, ROWS, WIDE = 128, 12, 16, 768
AUX, COLS, STATE = 1013, 768, 512
F32, BF16 = jnp.float32, jnp.bfloat16
VMEM = pltpu.VMEM


def node_tables():
    nodes = np.array([-1.0, -1.0 / np.sqrt(5.0), 1.0 / np.sqrt(5.0), 1.0])
    quadrature = np.array([1.0 / 6.0, 5.0 / 6.0, 5.0 / 6.0, 1.0 / 6.0])
    products = np.array(
        [np.prod([nodes[i] - nodes[k] for k in range(4) if k != i]) for i in range(4)]
    )
    derivative = np.zeros((4, 4))
    for i in range(4):
        for k in range(4):
            if i != k:
                derivative[i, k] = products[i] / (products[k] * (nodes[i] - nodes[k]))
            else:
                derivative[i, i] = sum(1.0 / (nodes[i] - nodes[m]) for m in range(4) if m != i)
    return derivative.astype(np.float32), quadrature.astype(np.float32)


def section_tables():
    d, w = node_tables()
    s = np.arange(8)
    up, j = s // 4, s % 4
    rows = []
    for p in range(2):
        i = 2 * p + up
        rows += [-d[i, up], -d[i, 1 - up], -d[i, 2 + up], -d[i, 3 - up]]
    rows += [-d[j, (j - shift) % 4] for shift in range(4)]
    rows += [w[2 * p + up] * w[j] for p in range(2)]
    return np.broadcast_to(np.stack(rows)[:, :, None], (14, 8, 128)).astype(np.float32).copy()


def sublane(shape):
    return lax.broadcasted_iota(jnp.int32, shape, len(shape) - 2)


def turn(x, shift):
    return pltpu.roll(x, shift % 8, axis=x.ndim - 2)


def pack_kernel(aux_ref, out_ref):
    row = lax.broadcasted_iota(jnp.int32, (512, 384), 0)
    lane = lax.broadcasted_iota(jnp.int32, (512, 384), 1)
    base, slot = row // ROWS * CAP, row % ROWS
    first = jnp.where((slot < CAP) & (lane == base + slot), 1.0, 0.0).astype(BF16)
    tail = aux_ref[WIDE:, :].astype(F32)
    tail = jnp.where(lax.broadcasted_iota(jnp.int32, tail.shape, 0) < AUX - WIDE, tail, 0.0).astype(BF16)
    nt = (((1,), (1,)), ((), ()))
    for part in range(3):
        rest = jnp.where((slot >= CAP) & (lane == base + slot - CAP + 4 * part), 1.0, 0.0).astype(BF16)
        piece = slice(256 * part, 256 * part + 256)
        out_ref[:, piece] = (
            lax.dot_general(first, aux_ref[piece, :], nt, preferred_element_type=F32)
            + lax.dot_general(rest, tail, nt, preferred_element_type=F32)
        ).astype(BF16)


def pack(aux_t):
    return pl.pallas_call(
        pack_kernel,
        grid=(4,),
        in_specs=[pl.BlockSpec((1024, 384), lambda g: (0, g))],
        out_specs=pl.BlockSpec((512, WIDE), lambda g: (g, 0)),
        out_shape=jax.ShapeDtypeStruct((DEV * ROWS, WIDE), BF16),
        compiler_params=pltpu.CompilerParams(vmem_limit_bytes=24 << 20),
        cost_estimate=pl.CostEstimate(flops=3_000_000_000, bytes_accessed=6_500_000, transcendentals=0),
    )(aux_t)


def section_kernel(tab_ref, prog_ref, mass_ref, sum_ref, edge_ref, state_ref, cells, sides):
    sub = sublane((EB, 8, LEV))
    j = sub % 4
    low = sub < 4
    is0, is3 = j == 0, j == 3

    def spread_row(a, _):
        tab = [tab_ref[k] for k in range(14)]
        weight = [tab[12 + p] * mass_ref[a, :, p] for p in range(2)]
        msum = []
        for p in range(2):
            t = weight[p] + turn(weight[p], 4)
            msum.append(1.0 / (t + turn(t, 7)))
        flow = [[weight[p] * prog_ref[f, a, :, p] for p in range(2)] for f in range(2)]
        for f in range(NF + 1):
            if f < NF:
                x = [prog_ref[f, a, :, p] for p in range(2)]
                xs = [turn(x[p], 4) for p in range(2)]
                value = []
                for p in range(2):
                    da = (
                        tab[4 * p] * x[0] + tab[4 * p + 1] * xs[0]
                        + tab[4 * p + 2] * x[1] + tab[4 * p + 3] * xs[1]
                    )
                    db = tab[8] * x[p]
                    for shift in range(1, 4):
                        moved = turn(x[p], shift)
                        moved = jnp.where(j >= shift, moved, turn(moved, 4))
                        db += tab[8 + shift] * moved
                    value.append(flow[0][p] * da + flow[1][p] * db)
                    t = weight[p] * x[p]
                    t = t + turn(t, 4)
                    t = (t + turn(t, 7)) * msum[p]
                    for b in range(EB):
                        for q in range(2):
                            cells[f, pl.ds(a * 32 + b * 4 + p * 2 + q, 1), :] = t[b, 2 * q : 2 * q + 1]
            else:
                value = weight
            for p in range(2):
                v = value[p]
                for up in range(2):
                    place = pl.ds(a * 4 + 2 * p + up, 1)
                    sides[0, f, place, :] = v[0, 4 * up : 4 * up + 1]
                    sides[1, f, place, :] = v[EB - 1, 4 * up + 3 : 4 * up + 4]
                after = jnp.concatenate([turn(v[:1] * 0.0, 0), turn(v[:-1], 5)], axis=0)
                before = jnp.concatenate([turn(v[1:], 3), v[:1] * 0.0], axis=0)
                sum_ref[f, a, :, p] = v + jnp.where(is0, after, jnp.where(is3, before, 0.0))
        return 0

    lax.fori_loop(0, EA, spread_row, 0)

    def join_rows(a, _):
        for f in range(NF + 1):
            here, there = sum_ref[f, a, :, 1], sum_ref[f, a + 1, :, 0]
            sum_ref[f, a, :, 1] = here + jnp.where(low, 0.0, turn(there, 4))
            sum_ref[f, a + 1, :, 0] = there + jnp.where(low, turn(here, 4), 0.0)
        return 0

    lax.fori_loop(0, EA - 1, join_rows, 0)
    row = lax.broadcasted_iota(jnp.int32, (EA * 4, LEV), 0)
    above, below = (row % 4 == 3) & (row < EA * 4 - 1), (row % 4 == 0) & (row > 0)
    for k in range(2):
        for f in range(NF + 1):
            v = sides[k, f]
            other = jnp.where(above, pltpu.roll(v, EA * 4 - 1, axis=0), jnp.where(below, pltpu.roll(v, 1, axis=0), 0.0))
            edge_ref[k, f] = (v + other).astype(BF16)
    for f in range(NF):
        state_ref[:, f * LEV : (f + 1) * LEV] = cells[f].astype(BF16)


def section(tab, prog, mass):
    return pl.pallas_call(
        section_kernel,
        in_specs=[pl.BlockSpec(memory_space=VMEM)] * 3,
        out_specs=[pl.BlockSpec(memory_space=VMEM)] * 3,
        out_shape=[
            jax.ShapeDtypeStruct((NF + 1, EA, EB, 2, 8, LEV), F32),
            jax.ShapeDtypeStruct((2, NF + 1, EA * 4, LEV), BF16),
            jax.ShapeDtypeStruct((COLS, STATE), BF16),
        ],
        scratch_shapes=[VMEM((NF, COLS, LEV), F32), VMEM((2, NF + 1, EA * 4, LEV), F32)],
        compiler_params=pltpu.CompilerParams(vmem_limit_bytes=40 << 20),
        cost_estimate=pl.CostEstimate(flops=20_000_000_000, bytes_accessed=16_000_000, transcendentals=0),
    )(tab, prog, mass)


def side_terms(sides, f, a, p):
    sub = sublane((8, LEV))
    low, j = sub < 4, sub % 4
    rows = [
        jnp.where(low, sides[k, f, pl.ds(a * 4 + 2 * p, 1), :], sides[k, f, pl.ds(a * 4 + 2 * p + 1, 1), :])
        for k in range(2)
    ]
    return jnp.where(j == 0, rows[0], 0.0), jnp.where(j == 3, rows[1], 0.0)


def rim_kernel(first_ref, last_ref, halo_ref, out_ref, sides):
    sides[...] = halo_ref[...].astype(F32)
    low = sublane((4, 8, LEV)) < 4
    for k, (ref, a, p) in enumerate(((first_ref, 0, 0), (last_ref, EA - 1, 1))):
        for f in range(NF + 1):
            left, right = side_terms(sides, f, a, p)
            rows = [ref[f, 0, b, 0] for b in range(EB)]
            rows[0] += left
            rows[-1] += right
            if p:
                rows = [turn(r, 4) for r in rows]
            packed = [jnp.where(low[0], rows[b], turn(rows[b + 1], 4)) for b in range(0, EB, 2)]
            out_ref[k, f * 32 : (f + 1) * 32] = jnp.concatenate(packed, axis=0).astype(BF16)


def rims(sums, halo):
    return pl.pallas_call(
        rim_kernel,
        grid=(1,),
        in_specs=[
            pl.BlockSpec((NF + 1, 1, EB, 1, 8, LEV), lambda g: (0, 0, 0, 0, 0, 0)),
            pl.BlockSpec((NF + 1, 1, EB, 1, 8, LEV), lambda g: (0, EA - 1, 0, 1, 0, 0)),
            pl.BlockSpec(halo.shape, lambda g: (0, 0, 0, 0)),
        ],
        out_specs=pl.BlockSpec((2, (NF + 1) * 32, LEV), lambda g: (0, 0, 0)),
        out_shape=jax.ShapeDtypeStruct((2, (NF + 1) * 32, LEV), BF16),
        scratch_shapes=[VMEM((2, NF + 1, EA * 4, LEV), F32)],
        compiler_params=pltpu.CompilerParams(vmem_limit_bytes=8 << 20),
    )(sums, sums, halo)


def close_kernel(sum_ref, prog_ref, halo_ref, rim_ref, out_ref, sides):
    sides[...] = halo_ref[...].astype(F32)
    low = sublane((8, LEV)) < 4

    def rim_terms(k, f):
        keep = low if k == 0 else jnp.logical_not(low)
        terms = []
        for pair in range(EB // 2):
            row = f * 32 + pair * 8
            both = rim_ref[k, row : row + 8].astype(F32)
            pieces = (both, turn(both, 4)) if k == 0 else (turn(both, 4), both)
            terms += [jnp.where(keep, piece, 0.0)[None] for piece in pieces]
        return jnp.concatenate(terms, axis=0)

    def close_half(a, p, rim):
        total = []
        for f in range(NF + 1):
            left, right = side_terms(sides, f, a, p)
            v = sum_ref[f, a, :, p]
            if rim is not None:
                v = v + rim_terms(rim, f)
            total.append(jnp.concatenate([v[:1] + left[None], v[1:-1], v[-1:] + right[None]], axis=0))
        scale = section_step / total[NF]
        for f in range(NF):
            out_ref[f, a, :, p] = prog_ref[f, a, :, p] + total[f] * scale

    def close_row(a, _):
        close_half(a, 0, None)
        close_half(a, 1, None)
        return 0

    close_half(0, 0, 0)
    close_half(0, 1, None)
    lax.fori_loop(1, EA - 1, close_row, 0)
    close_half(EA - 1, 0, None)
    close_half(EA - 1, 1, 1)


def close(sums, prog, halo, rim):
    return pl.pallas_call(
        close_kernel,
        in_specs=[pl.BlockSpec(memory_space=VMEM)] * 4,
        out_specs=pl.BlockSpec(memory_space=VMEM),
        out_shape=jax.ShapeDtypeStruct((NF, EA, EB, 2, 8, LEV), F32),
        scratch_shapes=[VMEM((2, NF + 1, EA * 4, LEV), F32)],
        compiler_params=pltpu.CompilerParams(vmem_limit_bytes=40 << 20),
        cost_estimate=pl.CostEstimate(flops=8_000_000_000, bytes_accessed=20_000_000, transcendentals=0),
    )(sums, prog, halo, rim)


def places_kernel(owner_ref, out_ref):
    owner = owner_ref[...]
    hit = sublane((DEV, COLS)) == owner
    hits = jnp.where(hit, 1.0, 0.0)
    lane = lax.broadcasted_iota(jnp.int32, (COLS, COLS), 1)
    before = jnp.where(sublane((COLS, COLS)) < lane, 1.0, 0.0).astype(BF16)
    earlier = jnp.dot(hits.astype(BF16), before, preferred_element_type=F32)
    slot = jnp.sum(hits * earlier, axis=0, keepdims=True).astype(jnp.int32)
    base = owner * ROWS
    none = jnp.full((1, COLS), -1, jnp.int32)
    rows = [base + slot]
    for part in range(3):
        rows.append(jnp.where(slot // 4 == part, base + CAP + slot - 4 * part, none))
    out_ref[...] = jnp.concatenate(rows + [none] * 4, axis=0)


def places(owner):
    return pl.pallas_call(
        places_kernel,
        in_specs=[pl.BlockSpec(memory_space=VMEM)],
        out_specs=pl.BlockSpec(memory_space=VMEM),
        out_shape=jax.ShapeDtypeStruct((8, COLS), jnp.int32),
        compiler_params=pltpu.CompilerParams(vmem_limit_bytes=16 << 20),
    )(owner)


def early_kernel(state_ref, win_ref, bias_ref, out_ref):
    out_ref[...] = jnp.dot(state_ref[...], win_ref[...], preferred_element_type=F32) + bias_ref[...]


def early(state, weight_in, bias_in):
    hid = weight_in.shape[1]
    return pl.pallas_call(
        early_kernel,
        grid=(4,),
        in_specs=[
            pl.BlockSpec((COLS, STATE), lambda g: (0, 0)),
            pl.BlockSpec((STATE, hid // 4), lambda g: (0, g)),
            pl.BlockSpec((1, hid // 4), lambda g: (0, g)),
        ],
        out_specs=pl.BlockSpec((COLS, hid // 4), lambda g: (0, g)),
        out_shape=jax.ShapeDtypeStruct((COLS, hid), F32),
        compiler_params=pltpu.CompilerParams(vmem_limit_bytes=24 << 20),
        cost_estimate=pl.CostEstimate(flops=2_000_000_000, bytes_accessed=10_000_000, transcendentals=0),
    )(state, weight_in, bias_in)


def tail_kernel(place_ref, home_ref, early_ref, win_ref, wout_ref, bout_ref, sec_ref, out_ref, inc):
    count = place_ref.shape[0]
    lane = lax.broadcasted_iota(jnp.int32, (count, DEV * ROWS), 1)

    def pick(k):
        return jnp.where(lane == place_ref[:, k : k + 1], 1.0, 0.0).astype(BF16)

    main = jnp.dot(pick(0), home_ref[...], preferred_element_type=F32).astype(BF16)
    rest = jnp.zeros((count, 256), F32)
    for part in range(3):
        rest += jnp.dot(pick(1 + part), home_ref[:, 256 * part : 256 * part + 256], preferred_element_type=F32)
    aux = jnp.concatenate([main, rest.astype(BF16)], axis=1)[:, :AUX]
    for half in range(2):
        cols = slice(1024 * half, 1024 * half + 1024)
        h = early_ref[:, cols] + jnp.dot(aux, win_ref[STATE:, cols], preferred_element_type=F32)
        h = (h / (1.0 + jnp.exp(-h))).astype(BF16)
        part = jnp.dot(h, wout_ref[cols, :], preferred_element_type=F32)
        total = part + bout_ref[...] if half == 0 else total + part
    total = total.astype(BF16).astype(F32)
    for f in range(NF):
        inc[f] = total[:, f * LEV : (f + 1) * LEV]
    rows_a = count // 32
    sub = sublane((8, LEV))
    right = sub % 4 >= 2
    for f in range(NF):

        def add(n, _):
            a, b = n // EB, n % EB
            for p in range(2):
                row = n * 4 + 2 * p
                term = jnp.where(right, inc[f, pl.ds(row + 1, 1), :], inc[f, pl.ds(row, 1), :])
                out_ref[f, a, b, p] = sec_ref[f, a, b, p] + term
            return 0

        lax.fori_loop(0, rows_a * EB, add, 0, unroll=8)


def tail(place, home, first, weight_in, weight_out, bias_out, sec):
    steps = 3
    count, rows_a = COLS // steps, EA // steps
    whole = pl.BlockSpec(memory_space=VMEM)
    block = pl.BlockSpec((NF, rows_a, EB, 2, 8, LEV), lambda g: (0, g, 0, 0, 0, 0))
    return pl.pallas_call(
        tail_kernel,
        grid=(steps,),
        in_specs=[
            pl.BlockSpec((count, 8), lambda g: (g, 0)),
            whole,
            pl.BlockSpec((count, first.shape[1]), lambda g: (g, 0)),
            whole,
            whole,
            whole,
            block,
        ],
        out_specs=block,
        out_shape=jax.ShapeDtypeStruct(sec.shape, F32),
        scratch_shapes=[VMEM((NF, count, LEV), F32)],
        compiler_params=pltpu.CompilerParams(vmem_limit_bytes=48 << 20),
        cost_estimate=pl.CostEstimate(flops=10_000_000_000, bytes_accessed=30_000_000, transcendentals=0),
    )(place, home, first, weight_in, weight_out, bias_out, sec)


def both_ways(pair, axis):
    count = lax.axis_size(axis)
    up = [(i, (i + 1) % count) for i in range(count)]
    down = [((i + 1) % count, i) for i in range(count)]
    return jnp.stack([lax.ppermute(pair[1], axis, up), lax.ppermute(pair[0], axis, down)])


def shards(prognostic, layer_mass, column_aux, group_owner, weight_in, bias_in, weight_out, bias_out):
    prog = prognostic.reshape(NF, EA, EB, 2, 8, LEV)
    mass = layer_mass.reshape(EA, EB, 2, 8, LEV)
    packed = pack(column_aux.T).reshape(DEV, ROWS, WIDE)
    home = lax.all_to_all(packed, ("curve", "sub"), split_axis=0, concat_axis=0, tiled=True)
    sums, edges, state = section(jnp.asarray(section_tables()), prog, mass)
    halo = both_ways(edges, "sub")
    place = places(group_owner.reshape(1, COLS)).T
    first = early(state, weight_in, bias_in[None])
    rim = both_ways(rims(sums, halo), "curve")
    sec = close(sums, prog, halo, rim)
    out = tail(place, home.reshape(DEV * ROWS, WIDE), first, weight_in, weight_out, bias_out[None], sec)
    return out.reshape(prognostic.shape)


def solution(mesh):
    return jax.shard_map(
        shards,
        mesh=mesh,
        in_specs=(
            P(None, "curve", "sub", None, None, None),
            P("curve", "sub", None, None, None),
            P(("curve", "sub"), None),
            P(("curve", "sub"), None),
            P(),
            P(),
            P(),
            P(),
        ),
        out_specs=P(None, "curve", "sub", None, None, None),
        check_vma=False,
    )
```

time: 203 us -> 110 us (0.54); the launches traced: 200 us -> 109 us
  other arithmetic: 83.8 us -> 0.04 us
  Pallas kernels: 0 us -> 49.9 us
  matrix products: 49.1 us -> 0 us
  local copies, waits for them, and re-layouts: 45.3 us -> 20.9 us
  waiting for transfers between devices: 4.18 us -> 18.3 us
  starting transfers between devices: 16.9 us -> 20 us
    pallas_call x0 -> x7, Pallas kernels: none -> 49.9 us  [the longest x1 25.1 us: tail(): pl.pallas_call(tail_kernel, grid=(steps,), in_specs=[pl.BlockSpec((count,...]
    dot_general x5 -> x0, matrix products: 49.1 us -> none  [the longest x1 17.5 us: advect(): jnp.einsum('ik,fabkjl->fabijl', derivative, prognostic, precision=lax.Pre...]
    add x4 -> x0, other arithmetic: 30.9 us -> none  [the longest x1 20.6 us: shards(): stacked[:, :, :, 0] + padded[:, :-2, :, 1]]
    ppermute x4, waiting for transfers between devices: 4.18 us -> 18.3 us  [the longest x2 18.3 us: both_ways(): lax.ppermute(pair[1], axis, up)]
    reduce_sum x2 -> x0, other arithmetic: 13.9 us -> none  [the longest x1 11 us: cell_average(): weighted_sum = jnp.sum(weighted, axis=(4, 6))]
    mul x3 -> x0, other arithmetic: 13.4 us -> none  [the longest x1 9.15 us: cell_average(): prognostic * node_weight[None]]
    reshape x2 -> x0, local copies, waits for them, and re-layouts: 13.2 us -> none  [the longest x1 6.64 us: shards(): relay(column_aux.reshape(devices, capacity, aux_width))]
    unnamed x34 -> x30, local copies, waits for them, and re-layouts: 7.64 us -> 20.7 us
  transfers between devices with their start and end apart: 5 -> 5, of which waited for: 2 -> 1; matrix products, arithmetic and copies ran while one was open for 38% -> 0% of each run, Pallas kernels for 0% -> 19%
where the time goes in v1:
time: 110 us; the launch traced here: 109 us
  Pallas kernels  49.9 us (45%)
  local copies, waits for them, and re-layouts  20.9 us (19%)
  starting transfers between devices  20 us (18%)
  waiting for transfers between devices  18.3 us (17%)
    pallas_call x1, Pallas kernels, tail(): pl.pallas_call(tail_kernel, grid=(steps,), in_specs=[pl.BlockSpec((count,...  25.1 us
    unnamed x30, local copies, waits for them, and re-layouts  20.7 us
    ppermute x2, waiting for transfers between devices, both_ways(): lax.ppermute(pair[1], axis, up)  18.3 us
    pallas_call x1, Pallas kernels, section(): pl.pallas_call(section_kernel, in_specs=[pl.BlockSpec(memory_space=VMEM)]...  12.6 us
    all_to_all x1, starting transfers between devices, shards(): lax.all_to_all(packed, ('curve', 'sub'), split_axis=0, concat_axis=0, til...  11.6 us
    ppermute x2, starting transfers between devices, both_ways(): lax.ppermute(pair[0], axis, down)  7.4 us
    pallas_call x1, Pallas kernels, close(): pl.pallas_call(close_kernel, in_specs=[pl.BlockSpec(memory_space=VMEM)] *...  4.51 us
    pallas_call x1, Pallas kernels, pack(): pl.pallas_call(pack_kernel, grid=(4,), in_specs=[pl.BlockSpec((1024, 384)...  4.41 us
  transfers between devices with their start and end apart: 5, of which 1 were waited for; matrix products, arithmetic and copies ran while one was open for 0% of the time, Pallas kernels for 19%

profile of v1, /device:TPU:0, one launch (start us, length us, event | category | flops | bytes accessed | tf_op | source)
XLA Modules:
  0.0 109.3 jit_solution(11795550829110507445)
XLA Ops:
  0.0 0.0 copy-start.7
  0.0 1.9 %copy-done.7 = bf16[1536,1013]{0,1:T(8,128)(2,1)S(1)} copy-done((bf16[1536,1013]{0,1:T(8,128)(2,1)S(1)}, bf16[1536,1013]{0,1:T(8,128)(2,1)}, u32[]{:S(2)}) %copy-start.7) | copy-done | bytes 3111960
  1.9 0.0 copy-start.11
  1.9 4.4 %shard_map.92 = bf16[2048,768]{1,0:T(8,128)(2,1)S(1)} custom-call(bf16[1013,1536]{1,0:T(8,128)(2,1)S(1)} %bitcast.30), custom_call_target="tpu_custom_call" | custom-call | flops 3000000000 | bytes 6500000 | tf_op jit(solution)/shard_map/pallas_call | solution.py:72
  6.3 0.0 copy-start.2
  6.3 1.7 %copy-done.2 = bf16[2048,768]{1,0:T(8,128)(2,1)} copy-done((bf16[2048,768]{1,0:T(8,128)(2,1)}, bf16[2048,768]{1,0:T(8,128)(2,1)S(1)}, u32[]{:S(2)}) %copy-start.2) | copy-done | bytes 3145752
  8.0 0.0 slice-start
  8.0 11.6 %all-to-all-start = ((bf16[128,16,768]{2,1,0:T(8,128)(2,1)}), bf16[128,16,768]{2,1,0:T(8,128)(2,1)}, u32[]{:S(2)}, u32[]{:S(2)}) async-start(bf16[128,16,768]{2,1,0:T(8,128)(2,1)} %bitcast.24), calls=%async_computation | async-start | bytes 6291456 | tf_op jit(solution)/shard_map/all_to_all | solution.py:380
  19.6 0.0 copy-done.11
  19.6 0.0 copy-start.5
  19.6 2.8 %copy-done.5 = f32[4,24,8,4,4,128]{5,4,3,2,1,0:T(4,128)S(1)} copy-done((f32[4,24,8,4,4,128]{5,4,3,2,1,0:T(4,128)S(1)}, f32[4,24,8,4,4,128]{5,4,3,2,1,0:T(4,128)}, u32[]{:S(2)}) %copy-start.5) | copy-done | bytes 6291480
  22.4 0.0 copy-start.9
  22.4 1.4 %copy-done.9 = f32[24,8,4,4,128]{4,3,2,1,0:T(4,128)S(1)} copy-done((f32[24,8,4,4,128]{4,3,2,1,0:T(4,128)S(1)}, f32[24,8,4,4,128]{4,3,2,1,0:T(4,128)}, u32[]{:S(2)}) %copy-start.9) | copy-done | bytes 1572888
  23.8 0.0 slice-start.1
  23.8 12.6 %shard_map.93 = (f32[5,24,8,2,8,128]{5,4,3,2,1,0:T(8,128)}, bf16[2,5,96,128]{3,2,1,0:T(8,128)(2,1)S(1)}, bf16[768,512]{1,0:T(8,128)(2,1)S(1)}) custom-call(f32[14,8,128]{2,1,0:T(8,128)S(1)} %copy-done.11, f32[4,24,8,2,8,128]{5,4,3,2,1,0:T(8,128)S(1)} %bitcast.28, f32[24,8,2,8,128]{4,3,2,1,0:T(8,128)S(1)} %bitcast.31), custom_call_target="tpu_custom_call" | custom-call | flops 20000000000 | bytes 16000000 | tf_op jit(solution)/shard_map/pallas_call | solution.py:154
  36.4 1.0 collective-permute-start
  37.4 2.3 %collective-permute-start.1 = (bf16[5,96,128]{2,1,0:T(8,128)(2,1)S(1)}, bf16[5,96,128]{2,1,0:T(8,128)(2,1)S(1)}, u32[]{:S(2)}, u32[]{:S(2)}) collective-permute-start(bf16[5,96,128]{2,1,0:T(8,128)(2,1)S(1)} %get-tuple-element.12), channel_id=1, source_target_pairs={{1,0},{2,1},{3,2},{0,3},{5,4},{6,5},{7,6},{4,7},{9,8},{10,9},{11,1... | collective-permute-start | bytes 368648 | tf_op jit(solution)/shard_map/ppermute | solution.py:373
  39.7 18.3 %collective-permute-done = bf16[5,96,128]{2,1,0:T(8,128)(2,1)S(1)} collective-permute-done((bf16[5,96,128]{2,1,0:T(8,128)(2,1)S(1)}, bf16[5,96,128]{2,1,0:T(8,128)(2,1)S(1)}, u32[]{:S(2)}, u32[]{:S(2)}) %collective-permute-start) | collective-permute-done | bytes 122912 | tf_op jit(solution)/shard_map/ppermute | solution.py:373
  58.0 0.0 collective-permute-done.1
  58.0 0.0 copy-start
  58.0 3.2 %copy-done = f32[5,24,8,2,8,128]{5,4,3,2,1,0:T(8,128)S(1)} copy-done((f32[5,24,8,2,8,128]{5,4,3,2,1,0:T(8,128)S(1)}, f32[5,24,8,2,8,128]{5,4,3,2,1,0:T(8,128)}, u32[]{:S(2)}) %copy-start) | copy-done | bytes 7864344
  61.2 0.0 copy-start.3
  61.3 0.1 collective-permute-start.2
  61.4 5.1 %collective-permute-start.3 = (bf16[160,128]{1,0:T(8,128)(2,1)S(1)}, bf16[160,128]{1,0:T(8,128)(2,1)S(1)}, u32[]{:S(2)}, u32[]{:S(2)}) collective-permute-start(bf16[160,128]{1,0:T(8,128)(2,1)S(1)} %get-tuple-element.14), channel_id=1, source_target_pairs={{4,0},{8,4},{12,8},{16,12},{20,16},{24,20},{28,24},{32,28},{36,32}... | collective-permute-start | bytes 122888 | tf_op jit(solution)/shard_map/ppermute | solution.py:373
  66.4 0.0 slice-done
  66.4 0.0 slice-done.1
  66.4 0.0 copy-done.3
  66.4 0.0 copy-start.4
  66.5 2.9 %shard_map.94.early_ref = f32[768,2048]{1,0:T(8,128)S(1)} custom-call(bf16[768,512]{1,0:T(8,128)(2,1)S(1)} %get-tuple-element.8.state_ref, bf16[1525,2048]{1,0:T(8,128)(2,1)S(1)} %bitcast.23, f32[1,2048]{1,0:T(1,128)S(1)} %bitcast.26), custom_call_target="tpu_custom_call" | custom-call | flops 2000000000 | bytes 10000000 | tf_op jit(solution)/shard_map/pallas_call | solution.py:292
  69.4 0.0 copy-start.1
  69.4 2.7 %copy-done.1 = f32[768,2048]{1,0:T(8,128)} copy-done((f32[768,2048]{1,0:T(8,128)}, f32[768,2048]{1,0:T(8,128)S(1)}, u32[]{:S(2)}) %copy-start.1) | copy-done | bytes 6291480
  72.0 0.0 copy-done.4
  72.1 0.3 shard_map.91
  72.4 0.2 copy.10
  72.6 0.0 collective-permute-done.2
  72.6 0.0 collective-permute-done.3
  72.6 0.0 copy-start.6
  72.6 2.8 %copy-done.6 = f32[4,24,8,4,4,128]{5,4,3,2,1,0:T(4,128)S(1)} copy-done((f32[4,24,8,4,4,128]{5,4,3,2,1,0:T(4,128)S(1)}, f32[4,24,8,4,4,128]{5,4,3,2,1,0:T(4,128)}, u32[]{:S(2)}) %copy-start.6) | copy-done | bytes 6291480
  75.4 0.0 copy-start.10
  75.4 4.5 %shard_map.96.sec_ref = f32[4,24,8,2,8,128]{5,4,3,2,1,0:T(8,128)S(1)} custom-call(f32[5,24,8,2,8,128]{5,4,3,2,1,0:T(8,128)} %get-tuple-element.9.first_ref.last_ref.sum_ref, f32[4,24,8,2,8,128]{5,4,3,2,1,0:T(8,128)S(1)} %bitcast.29, bf16[2,5,96,128]{3,2,1,0:T(8,128)(2,1)S(1)} %pad_maximum_fusion.halo_ref, bf16[2,160,128]{2,1,0:T(8,128)(2,1)S(1)} %pad_maximum_fusion.1.rim_ref), custom_call_target="tpu_custom_call" | custom-call | flops 8000000000 | bytes 20000000 | tf_op jit(solution)/shard_map/pallas_call | solution.py:249
  79.9 0.0 copy-start.12
  79.9 2.6 %copy-done.12 = f32[4,24,8,2,8,128]{5,4,3,2,1,0:T(8,128)} copy-done((f32[4,24,8,2,8,128]{5,4,3,2,1,0:T(8,128)}, f32[4,24,8,2,8,128]{5,4,3,2,1,0:T(8,128)S(1)}, u32[]{:S(2)}) %copy-start.12) | copy-done | bytes 6291480
  82.6 0.0 all-to-all-done
  82.6 0.0 copy-done.10
  82.6 0.0 copy-start.8
  82.6 1.6 %copy-done.8 = bf16[2048,512]{1,0:T(8,128)(2,1)S(1)} copy-done((bf16[2048,512]{1,0:T(8,128)(2,1)S(1)}, bf16[2048,512]{1,0:T(8,128)(2,1)}, u32[]{:S(2)}) %copy-start.8) | copy-done | bytes 2097176
  84.2 25.1 %shard_map.97 = f32[4,24,8,2,8,128]{5,4,3,2,1,0:T(8,128)} custom-call(s32[768,8]{1,0:T(8,128)S(1)} %bitcast.25, bf16[2048,768]{1,0:T(8,128)(2,1)} %bitcast.4.home_ref, f32[768,2048]{1,0:T(8,128)} %copy-done.1, bf16[1525,2048]{1,0:T(8,128)(2,1)} %win_ref.3, bf16[2048,512]{1,0:T(8,128)(2,1)S(1)} %copy-done.8, f32[1,512]{1,0:T(1,128)S(1)} %bitcast.32, ...), custom_call_target="tpu_custom_call" | custom-call | flops 10000000000 | bytes 30000000 | tf_op jit(solution)/shard_map/pallas_call | solution.py:349
  (6 shorter events, 0.1 us)
Async XLA Ops:
  0.0 1.9 %copy-start.7 = (bf16[1536,1013]{0,1:T(8,128)(2,1)S(1)}, bf16[1536,1013]{0,1:T(8,128)(2,1)}, u32[]{:S(2)}) copy-start(bf16[1536,1013]{0,1:T(8,128)(2,1)} %param.11) | copy-start | bytes 9335812
  1.9 17.7 %copy-start.11 = (f32[14,8,128]{2,1,0:T(8,128)S(1)}, f32[14,8,128]{2,1,0:T(8,128)}, u32[]{:S(2)}) copy-start(f32[14,8,128]{2,1,0:T(8,128)} %constant.2.clone.tab_ref) | copy-start | bytes 172036
  6.3 1.7 %copy-start.2 = (bf16[2048,768]{1,0:T(8,128)(2,1)}, bf16[2048,768]{1,0:T(8,128)(2,1)S(1)}, u32[]{:S(2)}) copy-start(bf16[2048,768]{1,0:T(8,128)(2,1)S(1)} %shard_map.92) | copy-start | bytes 9437188
  8.0 58.5 %slice-start = ((s8[6258688]{0:T(1024)(128)(4,1)}), s8[2064384]{0:T(1024)(128)(4,1)S(1)}, s32[]{:S(2)}) async-start(s8[6258688]{0:T(1024)(128)(4,1)} %bitcast.22), calls=%async_computation.1 | async-start | bytes 4128768
  8.0 74.6 %all-to-all-start = ((bf16[128,16,768]{2,1,0:T(8,128)(2,1)}), bf16[128,16,768]{2,1,0:T(8,128)(2,1)}, u32[]{:S(2)}, u32[]{:S(2)}) async-start(bf16[128,16,768]{2,1,0:T(8,128)(2,1)} %bitcast.24), calls=%async_computation | async-start | bytes 6291456 | tf_op jit(solution)/shard_map/all_to_all | solution.py:380
  19.6 2.8 %copy-start.5 = (f32[4,24,8,4,4,128]{5,4,3,2,1,0:T(4,128)S(1)}, f32[4,24,8,4,4,128]{5,4,3,2,1,0:T(4,128)}, u32[]{:S(2)}) copy-start(f32[4,24,8,4,4,128]{5,4,3,2,1,0:T(4,128)} %param.9) | copy-start | bytes 18874372
  22.4 1.4 %copy-start.9 = (f32[24,8,4,4,128]{4,3,2,1,0:T(4,128)S(1)}, f32[24,8,4,4,128]{4,3,2,1,0:T(4,128)}, u32[]{:S(2)}) copy-start(f32[24,8,4,4,128]{4,3,2,1,0:T(4,128)} %param.10) | copy-start | bytes 4718596
  23.8 42.6 %slice-start.1 = ((s8[6258688]{0:T(1024)(128)(4,1)}), s8[4194304]{0:T(1024)(128)(4,1)S(1)}, s32[]{:S(2)}) async-start(s8[6258688]{0:T(1024)(128)(4,1)} %bitcast.22), calls=%async_computation.2 | async-start | bytes 8388608
  36.4 21.6 %collective-permute-start = (bf16[5,96,128]{2,1,0:T(8,128)(2,1)S(1)}, bf16[5,96,128]{2,1,0:T(8,128)(2,1)S(1)}, u32[]{:S(2)}, u32[]{:S(2)}) collective-permute-start(bf16[5,96,128]{2,1,0:T(8,128)(2,1)S(1)} %get-tuple-element.11), channel_id=1, source_target_pairs={{0,1},{1,2},{2,3},{3,0},{4,5},{5,6},{6,7},{7,4},{8,9},{9,10},{10,1... | collective-permute-start | bytes 368648 | tf_op jit(solution)/shard_map/ppermute | solution.py:373
  37.4 20.6 %collective-permute-start.1 = (bf16[5,96,128]{2,1,0:T(8,128)(2,1)S(1)}, bf16[5,96,128]{2,1,0:T(8,128)(2,1)S(1)}, u32[]{:S(2)}, u32[]{:S(2)}) collective-permute-start(bf16[5,96,128]{2,1,0:T(8,128)(2,1)S(1)} %get-tuple-element.12), channel_id=1, source_target_pairs={{1,0},{2,1},{3,2},{0,3},{5,4},{6,5},{7,6},{4,7},{9,8},{10,9},{11,1... | collective-permute-start | bytes 368648 | tf_op jit(solution)/shard_map/ppermute | solution.py:373
  58.0 3.2 %copy-start = (f32[5,24,8,2,8,128]{5,4,3,2,1,0:T(8,128)S(1)}, f32[5,24,8,2,8,128]{5,4,3,2,1,0:T(8,128)}, u32[]{:S(2)}) copy-start(f32[5,24,8,2,8,128]{5,4,3,2,1,0:T(8,128)} %get-tuple-element.9.first_ref.last_ref.sum_ref) | copy-start | bytes 23592964
  61.2 5.2 %copy-start.3 = (f32[2048]{0:T(1024)S(1)}, f32[2048]{0:T(1024)}, u32[]{:S(2)}) copy-start(f32[2048]{0:T(1024)} %param.14) | copy-start | bytes 24580
  61.3 11.3 %collective-permute-start.2 = (bf16[160,128]{1,0:T(8,128)(2,1)S(1)}, bf16[160,128]{1,0:T(8,128)(2,1)S(1)}, u32[]{:S(2)}, u32[]{:S(2)}) collective-permute-start(bf16[160,128]{1,0:T(8,128)(2,1)S(1)} %get-tuple-element.13), channel_id=1, source_target_pairs={{0,4},{4,8},{8,12},{12,16},{16,20},{20,24},{24,28},{28,32},{32,36}... | collective-permute-start | bytes 122888 | tf_op jit(solution)/shard_map/ppermute | solution.py:373
  61.4 11.2 %collective-permute-start.3 = (bf16[160,128]{1,0:T(8,128)(2,1)S(1)}, bf16[160,128]{1,0:T(8,128)(2,1)S(1)}, u32[]{:S(2)}, u32[]{:S(2)}) collective-permute-start(bf16[160,128]{1,0:T(8,128)(2,1)S(1)} %get-tuple-element.14), channel_id=1, source_target_pairs={{4,0},{8,4},{12,8},{16,12},{20,16},{24,20},{28,24},{32,28},{36,32}... | collective-permute-start | bytes 122888 | tf_op jit(solution)/shard_map/ppermute | solution.py:373
  66.4 5.6 %copy-start.4 = (s32[768,1]{0,1:T(1,128)S(1)}, s32[768,1]{0,1:T(1,128)}, u32[]{:S(2)}) copy-start(s32[768,1]{0,1:T(1,128)} %param.12) | copy-start | bytes 9220
  69.4 2.7 %copy-start.1 = (f32[768,2048]{1,0:T(8,128)}, f32[768,2048]{1,0:T(8,128)S(1)}, u32[]{:S(2)}) copy-start(f32[768,2048]{1,0:T(8,128)S(1)} %shard_map.94.early_ref) | copy-start | bytes 18874372
  72.6 2.8 %copy-start.6 = (f32[4,24,8,4,4,128]{5,4,3,2,1,0:T(4,128)S(1)}, f32[4,24,8,4,4,128]{5,4,3,2,1,0:T(4,128)}, u32[]{:S(2)}) copy-start(f32[4,24,8,4,4,128]{5,4,3,2,1,0:T(4,128)} %param.9) | copy-start | bytes 18874372
  75.4 7.2 %copy-start.10 = (f32[512]{0:T(512)S(1)}, f32[512]{0:T(512)}, u32[]{:S(2)}) copy-start(f32[512]{0:T(512)} %param.16) | copy-start | bytes 6148
  79.9 2.7 %copy-start.12 = (f32[4,24,8,2,8,128]{5,4,3,2,1,0:T(8,128)}, f32[4,24,8,2,8,128]{5,4,3,2,1,0:T(8,128)S(1)}, u32[]{:S(2)}) copy-start(f32[4,24,8,2,8,128]{5,4,3,2,1,0:T(8,128)S(1)} %shard_map.96.sec_ref) | copy-start | bytes 18874372
  82.6 1.6 %copy-start.8 = (bf16[2048,512]{1,0:T(8,128)(2,1)S(1)}, bf16[2048,512]{1,0:T(8,128)(2,1)}, u32[]{:S(2)}) copy-start(bf16[2048,512]{1,0:T(8,128)(2,1)} %wout_ref.1) | copy-start | bytes 6291460

commit v2 on v1

v2 whole, which is shorter than its diff:
```python
import jax
import jax.numpy as jnp
import numpy as np
from jax import lax
from jax.experimental import pallas as pl
from jax.experimental.pallas import tpu as pltpu
from jax.sharding import PartitionSpec as P

section_step = 0.1
NF, EA, EB, LEV = 4, 24, 8, 128
DEV, CAP, ROWS, WIDE = 128, 12, 16, 768
AUX, COLS, STATE = 1013, 768, 512
F32, BF16 = jnp.float32, jnp.bfloat16
VMEM = pltpu.VMEM
GROUPS, GROUP = 4, 32
TURN = 53
TURN_BACK = pow(TURN, -1, DEV)


def node_tables():
    nodes = np.array([-1.0, -1.0 / np.sqrt(5.0), 1.0 / np.sqrt(5.0), 1.0])
    quadrature = np.array([1.0 / 6.0, 5.0 / 6.0, 5.0 / 6.0, 1.0 / 6.0])
    products = np.array(
        [np.prod([nodes[i] - nodes[k] for k in range(4) if k != i]) for i in range(4)]
    )
    derivative = np.zeros((4, 4))
    for i in range(4):
        for k in range(4):
            if i != k:
                derivative[i, k] = products[i] / (products[k] * (nodes[i] - nodes[k]))
            else:
                derivative[i, i] = sum(1.0 / (nodes[i] - nodes[m]) for m in range(4) if m != i)
    return derivative.astype(np.float32), quadrature.astype(np.float32)


def section_tables():
    d, w = node_tables()
    s = np.arange(8)
    up, j = s // 4, s % 4
    rows = []
    for p in range(2):
        i = 2 * p + up
        rows += [-d[i, up], -d[i, 1 - up], -d[i, 2 + up], -d[i, 3 - up]]
    rows += [-d[j, (j - shift) % 4] for shift in range(4)]
    rows += [w[2 * p + up] * w[j] for p in range(2)]
    return np.broadcast_to(np.stack(rows)[:, :, None], (14, 8, 128)).astype(np.float32).copy()


def sublane(shape):
    return lax.broadcasted_iota(jnp.int32, shape, len(shape) - 2)


def turn(x, shift):
    return pltpu.roll(x, shift % 8, axis=x.ndim - 2)


def pack_kernel(aux_ref, out_ref):
    row = lax.broadcasted_iota(jnp.int32, (512, 384), 0)
    lane = lax.broadcasted_iota(jnp.int32, (512, 384), 1)
    base, slot = row // ROWS * CAP, row % ROWS
    first = jnp.where((slot < CAP) & (lane == base + slot), 1.0, 0.0).astype(BF16)
    tail = aux_ref[WIDE:, :].astype(F32)
    tail = jnp.where(lax.broadcasted_iota(jnp.int32, tail.shape, 0) < AUX - WIDE, tail, 0.0).astype(BF16)
    nt = (((1,), (1,)), ((), ()))
    for part in range(3):
        rest = jnp.where((slot >= CAP) & (lane == base + slot - CAP + 4 * part), 1.0, 0.0).astype(BF16)
        piece = slice(256 * part, 256 * part + 256)
        out_ref[:, piece] = (
            lax.dot_general(first, aux_ref[piece, :], nt, preferred_element_type=F32)
            + lax.dot_general(rest, tail, nt, preferred_element_type=F32)
        ).astype(BF16)


def pack(aux_t):
    return pl.pallas_call(
        pack_kernel,
        grid=(4,),
        in_specs=[pl.BlockSpec((1024, 384), lambda g: (0, g))],
        out_specs=pl.BlockSpec((512, WIDE), lambda g: (g, 0)),
        out_shape=jax.ShapeDtypeStruct((DEV * ROWS, WIDE), BF16),
        compiler_params=pltpu.CompilerParams(vmem_limit_bytes=24 << 20),
        cost_estimate=pl.CostEstimate(flops=3_000_000_000, bytes_accessed=6_500_000, transcendentals=0),
    )(aux_t)


def section_rows(tab_ref, sec, mass, sums, sides, cells):
    sub = sublane((EB, 8, LEV))
    j = sub % 4
    low = sub < 4
    is0, is3 = j == 0, j == 3

    def spread_row(a, _):
        tab = [tab_ref[k] for k in range(14)]
        weight = [tab[12 + p] * mass[a, :, p] for p in range(2)]
        msum = []
        for p in range(2):
            t = weight[p] + turn(weight[p], 4)
            msum.append(1.0 / (t + turn(t, 7)))
        flow = [[weight[p] * sec[f, a, :, p] for p in range(2)] for f in range(2)]
        for f in range(NF + 1):
            if f < NF:
                x = [sec[f, a, :, p] for p in range(2)]
                xs = [turn(x[p], 4) for p in range(2)]
                value = []
                for p in range(2):
                    da = (
                        tab[4 * p] * x[0] + tab[4 * p + 1] * xs[0]
                        + tab[4 * p + 2] * x[1] + tab[4 * p + 3] * xs[1]
                    )
                    db = tab[8] * x[p]
                    for shift in range(1, 4):
                        moved = turn(x[p], shift)
                        moved = jnp.where(j >= shift, moved, turn(moved, 4))
                        db += tab[8 + shift] * moved
                    value.append(flow[0][p] * da + flow[1][p] * db)
                    t = weight[p] * x[p]
                    t = t + turn(t, 4)
                    t = (t + turn(t, 7)) * msum[p]
                    for b in range(EB):
                        for q in range(2):
                            cells[f, pl.ds(a * 32 + b * 4 + p * 2 + q, 1), :] = t[b, 2 * q : 2 * q + 1]
            else:
                value = weight
            for p in range(2):
                v = value[p]
                for up in range(2):
                    place = pl.ds(a * 4 + 2 * p + up, 1)
                    sides[0, f, place, :] = v[0, 4 * up : 4 * up + 1]
                    sides[1, f, place, :] = v[EB - 1, 4 * up + 3 : 4 * up + 4]
                none = jnp.zeros((1, 8, LEV), F32)
                after = jnp.concatenate([none, turn(v[:-1], 5)], axis=0)
                before = jnp.concatenate([turn(v[1:], 3), none], axis=0)
                sums[f, a, :, p] = v + jnp.where(is0, after, jnp.where(is3, before, 0.0))
        return 0

    lax.fori_loop(0, EA, spread_row, 0)

    def join_rows(a, _):
        for f in range(NF + 1):
            here, there = sums[f, a, :, 1], sums[f, a + 1, :, 0]
            sums[f, a, :, 1] = here + jnp.where(low, 0.0, turn(there, 4))
            sums[f, a + 1, :, 0] = there + jnp.where(low, turn(here, 4), 0.0)
        return 0

    lax.fori_loop(0, EA - 1, join_rows, 0)


def side_edges(sides, edge):
    row = lax.broadcasted_iota(jnp.int32, (EA * 4, LEV), 0)
    above, below = (row % 4 == 3) & (row < EA * 4 - 1), (row % 4 == 0) & (row > 0)
    for k in range(2):
        for f in range(NF + 1):
            v = sides[k, f]
            up, down = pltpu.roll(v, EA * 4 - 1, axis=0), pltpu.roll(v, 1, axis=0)
            edge[k, f] = (v + jnp.where(above, up, jnp.where(below, down, 0.0))).astype(BF16)


def side_terms(sides, f, a, p):
    sub = sublane((8, LEV))
    low, j = sub < 4, sub % 4
    rows = [
        jnp.where(low, sides[k, f, pl.ds(a * 4 + 2 * p, 1), :], sides[k, f, pl.ds(a * 4 + 2 * p + 1, 1), :])
        for k in range(2)
    ]
    return jnp.where(j == 0, rows[0], 0.0), jnp.where(j == 3, rows[1], 0.0)


def rim_rows(sums, sides, rim):
    low = sublane((8, LEV)) < 4
    for k, (a, p) in enumerate(((0, 0), (EA - 1, 1))):
        for f in range(NF + 1):
            left, right = side_terms(sides, f, a, p)
            rows = [sums[f, a, b, p] for b in range(EB)]
            rows[0] += left
            rows[-1] += right
            if p:
                rows = [turn(r, 4) for r in rows]
            packed = [jnp.where(low, rows[b], turn(rows[b + 1], 4)) for b in range(0, EB, 2)]
            rim[k, f * 32 : (f + 1) * 32] = jnp.concatenate(packed, axis=0).astype(BF16)


def close_rows(sums, sides, rim, sec):
    low = sublane((8, LEV)) < 4

    def rim_terms(k, f):
        keep = low if k == 0 else jnp.logical_not(low)
        terms = []
        for pair in range(EB // 2):
            row = f * 32 + pair * 8
            both = rim[k, row : row + 8].astype(F32)
            pieces = (both, turn(both, 4)) if k == 0 else (turn(both, 4), both)
            terms += [jnp.where(keep, piece, 0.0)[None] for piece in pieces]
        return jnp.concatenate(terms, axis=0)

    for k, (a, p) in enumerate(((0, 0), (EA - 1, 1))):
        for f in range(NF + 1):
            sums[f, a, :, p] += rim_terms(k, f)

    def close_row(a, _):
        for p in range(2):
            total = []
            for f in range(NF + 1):
                left, right = side_terms(sides, f, a, p)
                v = sums[f, a, :, p]
                total.append(jnp.concatenate([v[:1] + left[None], v[1:-1], v[-1:] + right[None]], axis=0))
            scale = section_step / total[NF]
            for f in range(NF):
                sec[f, a, :, p] += total[f] * scale
        return 0

    lax.fori_loop(0, EA, close_row, 0)


def find_places(owner_ref, mine, out):
    curve, x = mine
    owner = owner_ref[...]
    there = owner // 4
    rel = (
        (x - owner % 4) % 4
        + (curve // 8 - there // 8) % 4 * 4
        + (curve // 2 - there // 2) % 4 * 16
        + (curve - there) % 2 * 64
    )
    order = rel * TURN_BACK % DEV
    hits = jnp.where(sublane((DEV, COLS)) == order, 1.0, 0.0)
    lane = lax.broadcasted_iota(jnp.int32, (COLS, COLS), 1)
    before = jnp.where(sublane((COLS, COLS)) < lane, 1.0, 0.0).astype(BF16)
    earlier = jnp.dot(hits.astype(BF16), before, preferred_element_type=F32)
    slot = jnp.sum(hits * earlier, axis=0, keepdims=True)
    base = order.astype(F32) * ROWS
    none = jnp.full((1, COLS), -1.0, F32)
    rows = [base + slot]
    for part in range(3):
        inside = (slot >= 4 * part) & (slot < 4 * part + 4)
        rows.append(jnp.where(inside, base + CAP + slot - 4 * part, none))
    out[...] = jnp.transpose(jnp.concatenate(rows + [none] * 4, axis=0)).astype(jnp.int32)


def exchange_kernel(
    tab_ref, send_ref, owner_ref, bias_ref, prog_ref, mass_ref, win_ref, sec_out, early_out, aux_out,
    sec, mass, sums, sides, cells, home, win, early, state, acc, places, edge, edge_in, rim, rim_in,
    load_sem, store_sem, self_sem, send_sem, recv_sem, edge_send, edge_recv, rim_send, rim_recv,
):
    curve, x = lax.axis_index("curve"), lax.axis_index("sub")
    y, z, core = curve // 8, curve // 2 % 4, curve % 2
    me = curve * 4 + x
    mesh = pl.DeviceIdType.MESH

    loads = [
        pltpu.make_async_copy(prog_ref, sec, load_sem.at[0]),
        pltpu.make_async_copy(mass_ref, mass, load_sem.at[1]),
        pltpu.make_async_copy(win_ref.at[pl.ds(0, STATE)], win, load_sem.at[2]),
    ]
    for load in loads:
        load.start()

    barrier = pltpu.get_barrier_semaphore()

    def greet(d, _):
        t = lax.rem(me + d, DEV)
        pl.semaphore_signal(barrier, inc=1, device_id={"curve": t // 4, "sub": lax.rem(t, 4)}, device_id_type=mesh)
        return 0

    lax.fori_loop(1, DEV, greet, 0)
    pl.semaphore_wait(barrier, DEV - 1)

    own = pltpu.make_async_copy(send_ref.at[me], home.at[0], self_sem)
    own.start()

    def send_group(g):
        def send(o, _):
            rel = lax.rem(o * TURN, DEV)
            to_x = lax.rem(x + rel % 4, 4)
            to_curve = (
                lax.rem(y + rel // 4 % 4, 4) * 8 + lax.rem(z + rel // 16 % 4, 4) * 2 + lax.rem(core + rel // 64, 2)
            )
            pltpu.make_async_remote_copy(
                send_ref.at[to_curve * 4 + to_x], home.at[o], send_sem.at[g], recv_sem.at[g],
                device_id={"curve": to_curve, "sub": to_x}, device_id_type=mesh,
            ).start()
            return 0

        lax.fori_loop(max(1, GROUP * g), GROUP * g + GROUP, send, 0)

    def group_copy(g):
        span = pl.ds(max(1, GROUP * g), GROUP - (g == 0))
        return pltpu.make_async_remote_copy(
            send_ref.at[span], home.at[span], send_sem.at[g], recv_sem.at[g],
            device_id={"curve": curve, "sub": x}, device_id_type=mesh,
        )

    def select_group(g):
        group_copy(g).wait_recv()
        if g == 0:
            own.wait()

        def chunk(m, _):
            rows = pl.ds(m * 256, 256)
            lane = lax.broadcasted_iota(jnp.int32, (256, GROUP * ROWS), 1) + GROUP * ROWS * g

            def pick(k):
                return jnp.where(lane == places[rows, k : k + 1], 1.0, 0.0).astype(BF16)

            def block(lanes):
                return home[GROUP * g : GROUP * (g + 1), :, lanes].reshape(GROUP * ROWS, -1)

            main = jnp.dot(pick(0), block(slice(0, WIDE)), preferred_element_type=F32)
            rest = jnp.dot(pick(1), block(slice(0, 256)), preferred_element_type=F32)
            for part in range(1, 3):
                rest += jnp.dot(
                    pick(1 + part), block(slice(256 * part, 256 * part + 256)), preferred_element_type=F32
                )
            if g:
                main, rest = main + acc[rows, :WIDE], rest + acc[rows, WIDE:]
            if g < GROUPS - 1:
                acc[rows, :WIDE], acc[rows, WIDE:] = main, rest
            else:
                aux_out[rows, :WIDE], aux_out[rows, WIDE:] = main.astype(BF16), rest.astype(BF16)
            return 0

        lax.fori_loop(0, COLS // 256, chunk, 0)

    def both_ways(src, dst, send, recv, axis, place, count):
        return [
            pltpu.make_async_remote_copy(
                src.at[k], dst.at[1 - k], send.at[k], recv.at[1 - k],
                device_id={axis: lax.rem(place + (1 if k else count - 1), count)}, device_id_type=mesh,
            )
            for k in range(2)
        ]

    def await_both(copies):
        for copy in copies:
            copy.wait_recv()

    send_group(0)
    send_group(1)
    loads[0].wait()
    loads[1].wait()
    section_rows(tab_ref, sec, mass, sums, sides, cells)
    side_edges(sides, edge)
    edge_copies = both_ways(edge, edge_in, edge_send, edge_recv, "sub", x, 4)
    for copy in edge_copies:
        copy.start()
    send_group(2)

    for f in range(NF):
        state[:, f * LEV : (f + 1) * LEV] = cells[f].astype(BF16)
    find_places(owner_ref, (curve, x), places)
    loads[2].wait()

    def early_tile(t, _):
        lanes = pl.ds(pl.multiple_of(t * 256, 256), 256)
        early[:, lanes] = jnp.dot(state[...], win[:, lanes], preferred_element_type=F32) + bias_ref[:, lanes]
        return 0

    lax.fori_loop(0, early.shape[1] // 256, early_tile, 0)
    early_store = pltpu.make_async_copy(early, early_out, store_sem.at[0])
    early_store.start()

    await_both(edge_copies)
    sides[...] = edge_in[...].astype(F32)
    rim_rows(sums, sides, rim)
    rim_copies = both_ways(rim, rim_in, rim_send, rim_recv, "curve", curve, 32)
    for copy in rim_copies:
        copy.start()
    send_group(3)

    select_group(0)
    select_group(1)
    await_both(rim_copies)
    close_rows(sums, sides, rim_in, sec)
    sec_store = pltpu.make_async_copy(sec, sec_out, store_sem.at[1])
    sec_store.start()
    select_group(2)
    select_group(3)
    for g in range(GROUPS):
        group_copy(g).wait_send()
    for copy in edge_copies + rim_copies:
        copy.wait_send()
    early_store.wait()
    sec_store.wait()


def exchange(tab, packed, owner, bias_in, prog, mass, weight_in):
    hid = weight_in.shape[1]
    vm, hbm = pl.BlockSpec(memory_space=VMEM), pl.BlockSpec(memory_space=pl.ANY)
    dma = pltpu.SemaphoreType.DMA
    return pl.pallas_call(
        exchange_kernel,
        in_specs=[vm, vm, vm, vm, hbm, hbm, hbm],
        out_specs=[hbm, hbm, vm],
        out_shape=[
            jax.ShapeDtypeStruct(prog.shape, F32),
            jax.ShapeDtypeStruct((COLS, hid), F32),
            jax.ShapeDtypeStruct((COLS, WIDE + 256), BF16),
        ],
        scratch_shapes=[
            VMEM(prog.shape, F32),
            VMEM(mass.shape, F32),
            VMEM((NF + 1, EA, EB, 2, 8, LEV), F32),
            VMEM((2, NF + 1, EA * 4, LEV), F32),
            VMEM((NF, COLS, LEV), F32),
            VMEM((DEV, ROWS, WIDE), BF16),
            VMEM((STATE, hid), BF16),
            VMEM((COLS, hid), F32),
            VMEM((COLS, STATE), BF16),
            VMEM((COLS, WIDE + 256), F32),
            VMEM((COLS, 8), jnp.int32),
            VMEM((2, NF + 1, EA * 4, LEV), BF16),
            VMEM((2, NF + 1, EA * 4, LEV), BF16),
            VMEM((2, (NF + 1) * 32, LEV), BF16),
            VMEM((2, (NF + 1) * 32, LEV), BF16),
            dma((3,)), dma((2,)), dma, dma((GROUPS,)), dma((GROUPS,)), dma((2,)), dma((2,)), dma((2,)), dma((2,)),
        ],
        compiler_params=pltpu.CompilerParams(
            collective_id=1, has_side_effects=True, vmem_limit_bytes=56 << 20
        ),
        cost_estimate=pl.CostEstimate(flops=10_000_000_000, bytes_accessed=40_000_000, transcendentals=0),
    )(tab, packed, owner, bias_in, prog, mass, weight_in)


def tail_kernel(
    aux_ref, early_ref, wa_ref, wb_ref, wout_ref, bout_ref, sec_ref, out_ref, sec, inc, total, load_sem, store_sem
):
    step = pl.program_id(0)
    rows_a = 4
    pieces = [pl.ds(n * rows_a, rows_a) for n in range(EA // rows_a)]

    @pl.when(step == 0)
    def _():
        pltpu.make_async_copy(sec_ref, sec, load_sem).start()

    h = (
        early_ref[...]
        + jnp.dot(aux_ref[:, :STATE], wa_ref[...], preferred_element_type=F32)
        + jnp.dot(aux_ref[:, STATE:AUX], wb_ref[: AUX - STATE, :], preferred_element_type=F32)
    )
    h = (h / (1.0 + jnp.exp(-h))).astype(BF16)
    part = jnp.dot(h, wout_ref[...], preferred_element_type=F32)

    @pl.when(step == 0)
    def _():
        total[...] = part + bout_ref[...]

    @pl.when(step > 0)
    def _():
        total[...] += part

    @pl.when(step == pl.num_programs(0) - 1)
    def _():
        pltpu.make_async_copy(sec_ref, sec, load_sem).wait()
        right = sublane((8, LEV)) % 4 >= 2
        stores = []
        for n, piece in enumerate(pieces):
            count = rows_a * 32
            for f in range(NF):
                inc[f] = total[n * count : (n + 1) * count, f * LEV : (f + 1) * LEV].astype(BF16).astype(F32)
                for e in range(rows_a * EB):
                    for p in range(2):
                        row = e * 4 + 2 * p
                        term = jnp.where(right, inc[f, row + 1 : row + 2, :], inc[f, row : row + 1, :])
                        sec[f, n * rows_a + e // EB, e % EB, p] += term
            store = pltpu.make_async_copy(sec.at[:, piece], out_ref.at[:, piece], store_sem.at[n])
            store.start()
            stores.append(store)
        for store in stores:
            store.wait()


def tail(aux, early, weight_in, weight_out, bias_out, sec):
    steps = 4
    hid = early.shape[1]
    tile = hid // steps
    hbm = pl.BlockSpec(memory_space=pl.ANY)
    return pl.pallas_call(
        tail_kernel,
        grid=(steps,),
        in_specs=[
            pl.BlockSpec(aux.shape, lambda t: (0, 0)),
            pl.BlockSpec((COLS, tile), lambda t: (0, t)),
            pl.BlockSpec((STATE, tile), lambda t: (1, t)),
            pl.BlockSpec((STATE, tile), lambda t: (2, t)),
            pl.BlockSpec((tile, STATE), lambda t: (t, 0)),
            pl.BlockSpec((1, STATE), lambda t: (0, 0)),
            hbm,
        ],
        out_specs=hbm,
        out_shape=jax.ShapeDtypeStruct(sec.shape, F32),
        scratch_shapes=[
            VMEM(sec.shape, F32),
            VMEM((NF, 128, LEV), F32),
            VMEM((COLS, STATE), F32),
            pltpu.SemaphoreType.DMA,
            pltpu.SemaphoreType.DMA((EA // 4,)),
        ],
        compiler_params=pltpu.CompilerParams(vmem_limit_bytes=40 << 20),
        cost_estimate=pl.CostEstimate(flops=5_000_000_000, bytes_accessed=30_000_000, transcendentals=0),
    )(aux, early, weight_in, weight_in, weight_out, bias_out, sec)


def shards(prognostic, layer_mass, column_aux, group_owner, weight_in, bias_in, weight_out, bias_out):
    prog = prognostic.reshape(NF, EA, EB, 2, 8, LEV)
    mass = layer_mass.reshape(EA, EB, 2, 8, LEV)
    packed = pack(column_aux.T).reshape(DEV, ROWS, WIDE)
    sec, early, aux = exchange(
        jnp.asarray(section_tables()), packed, group_owner.reshape(1, COLS), bias_in[None], prog, mass, weight_in
    )
    out = tail(aux, early, weight_in, weight_out, bias_out[None], sec)
    return out.reshape(prognostic.shape)


def solution(mesh):
    return jax.shard_map(
        shards,
        mesh=mesh,
        in_specs=(
            P(None, "curve", "sub", None, None, None),
            P("curve", "sub", None, None, None),
            P(("curve", "sub"), None),
            P(("curve", "sub"), None),
            P(),
            P(),
            P(),
            P(),
        ),
        out_specs=P(None, "curve", "sub", None, None, None),
        check_vma=False,
    )
```

time: 110 us -> 79.4 us (0.72)
  Pallas kernels: 49.9 us -> 72 us
  starting transfers between devices: 20 us -> 0 us
  waiting for transfers between devices: 18.3 us -> 0 us
  local copies, waits for them, and re-layouts: 20.9 us -> 6.55 us
    pallas_call x6 -> x2, Pallas kernels: 45.5 us -> 67.6 us  [the longest x1 55.1 us: exchange(): pl.pallas_call(exchange_kernel, in_specs=[vm, vm, vm, vm, hbm, hbm, hbm],...]
    ppermute x4 -> x0, waiting for transfers between devices: 18.3 us -> none  [the longest x2 18.3 us: both_ways(): lax.ppermute(pair[1], axis, up)]
    unnamed x30 -> x14, local copies, waits for them, and re-layouts: 20.7 us -> 6.55 us
    all_to_all x1 -> x0, starting transfers between devices: 11.6 us -> none  [shards(): lax.all_to_all(packed, ('curve', 'sub'), split_axis=0, concat_axis=0, til...]
    ppermute x4 -> x0, starting transfers between devices: 8.43 us -> none  [the longest x2 7.4 us: both_ways(): lax.ppermute(pair[0], axis, down)]
  transfers between devices with their start and end apart: 5 -> 0, of which waited for: 1 -> 0; matrix products, arithmetic and copies ran while one was open for 0% -> 0% of each run, Pallas kernels for 19% -> 0%
where the time goes in v2:
time: 79.4 us; the launch traced here: 78.6 us
  Pallas kernels  72 us (91%)
  local copies, waits for them, and re-layouts  6.55 us (8%)
    pallas_call x1, Pallas kernels, exchange(): pl.pallas_call(exchange_kernel, in_specs=[vm, vm, vm, vm, hbm, hbm, hbm],...  55.1 us
    pallas_call x1, Pallas kernels, tail(): pl.pallas_call(tail_kernel, grid=(steps,), in_specs=[pl.BlockSpec(aux.sha...  12.4 us
    unnamed x14, local copies, waits for them, and re-layouts  6.55 us
    pallas_call x1, Pallas kernels, pack(): pl.pallas_call(pack_kernel, grid=(4,), in_specs=[pl.BlockSpec((1024, 384)...  4.41 us

profile of v2, /device:TPU:0, one launch (start us, length us, event | category | flops | bytes accessed | tf_op | source)
XLA Modules:
  0.0 78.6 jit_solution(7876792992643067023)
XLA Ops:
  0.0 0.0 copy-start.3
  0.0 1.9 %copy-done.3 = bf16[1536,1013]{0,1:T(8,128)(2,1)S(1)} copy-done((bf16[1536,1013]{0,1:T(8,128)(2,1)S(1)}, bf16[1536,1013]{0,1:T(8,128)(2,1)}, u32[]{:S(2)}) %copy-start.3) | copy-done | bytes 3111960
  1.9 0.0 slice-start
  1.9 4.4 %shard_map.91 = bf16[2048,768]{1,0:T(8,128)(2,1)S(1)} custom-call(bf16[1013,1536]{1,0:T(8,128)(2,1)S(1)} %bitcast.11), custom_call_target="tpu_custom_call" | custom-call | flops 3000000000 | bytes 6500000 | tf_op jit(solution)/shard_map/pallas_call | solution.py:75
  6.3 0.0 copy-start.4
  6.3 1.7 %copy-done.4 = bf16[2048,768]{1,0:T(8,128)(2,1)} copy-done((bf16[2048,768]{1,0:T(8,128)(2,1)}, bf16[2048,768]{1,0:T(8,128)(2,1)S(1)}, u32[]{:S(2)}) %copy-start.4) | copy-done | bytes 3145752
  8.0 0.0 slice-start.1
  8.0 0.0 copy-start.2
  8.0 55.1 %shard_map.92 = (f32[4,24,8,2,8,128]{5,4,3,2,1,0:T(8,128)}, f32[768,2048]{1,0:T(8,128)}, bf16[768,1024]{1,0:T(8,128)(2,1)}) custom-call(f32[14,8,128]{2,1,0:T(8,128)} %constant.2.clone.tab_ref, bf16[128,16,768]{2,1,0:T(8,128)(2,1)} %bitcast.12, s32[1,768]{1,0:T(1,128)} %bitcast.16, f32[1,2048]{1,0:T(1,128)} %bitcast.15, f32[4,24,8,2,8,128]{5,4,3,2,1,0:T(8,128)} %bitcast.13, ...), custom_call_target="tpu_custom_call" | custom-call | flops 10000000000 | bytes 40000000 | tf_op jit(solution)/shard_map/pallas_call | solution.py:389
  63.1 0.0 slice-done
  63.1 0.0 slice-done.1
  63.1 0.0 copy-done.2
  63.1 0.0 copy-start
  63.2 1.6 %copy-done = bf16[2048,512]{1,0:T(8,128)(2,1)S(1)} copy-done((bf16[2048,512]{1,0:T(8,128)(2,1)S(1)}, bf16[2048,512]{1,0:T(8,128)(2,1)}, u32[]{:S(2)}) %copy-start) | copy-done | bytes 2097176
  64.7 0.0 copy-start.1
  64.7 1.4 %copy-done.1 = bf16[768,1024]{1,0:T(8,128)(2,1)S(1)} copy-done((bf16[768,1024]{1,0:T(8,128)(2,1)S(1)}, bf16[768,1024]{1,0:T(8,128)(2,1)}, u32[]{:S(2)}) %copy-start.1) | copy-done | bytes 1572888
  66.1 12.4 %shard_map.93 = f32[4,24,8,2,8,128]{5,4,3,2,1,0:T(8,128)} custom-call(bf16[768,1024]{1,0:T(8,128)(2,1)S(1)} %copy-done.1, f32[768,2048]{1,0:T(8,128)} %get-tuple-element.9.early_ref, bf16[1525,2048]{1,0:T(8,128)(2,1)S(1)} %bitcast.9, bf16[1525,2048]{1,0:T(8,128)(2,1)S(1)} %bitcast.9, bf16[2048,512]{1,0:T(8,128)(2,1)S(1)} %copy-done, f32[1,512]{1,0:T(1,128)S(1)} %bitcast.10, ...), custom_call_target="tpu_custom_call" | custom-call | flops 5000000000 | bytes 30000000 | tf_op jit(solution)/shard_map/pallas_call | solution.py:476
  (1 shorter events, 0.0 us)
Async XLA Ops:
  0.0 1.9 %copy-start.3 = (bf16[1536,1013]{0,1:T(8,128)(2,1)S(1)}, bf16[1536,1013]{0,1:T(8,128)(2,1)}, u32[]{:S(2)}) copy-start(bf16[1536,1013]{0,1:T(8,128)(2,1)} %param.11) | copy-start | bytes 9335812
  1.9 61.2 %slice-start = ((s8[6258688]{0:T(1024)(128)(4,1)}), s8[4194304]{0:T(1024)(128)(4,1)S(1)}, s32[]{:S(2)}) async-start(s8[6258688]{0:T(1024)(128)(4,1)} %bitcast.8), calls=%async_computation | async-start | bytes 8388608
  6.3 1.7 %copy-start.4 = (bf16[2048,768]{1,0:T(8,128)(2,1)}, bf16[2048,768]{1,0:T(8,128)(2,1)S(1)}, u32[]{:S(2)}) copy-start(bf16[2048,768]{1,0:T(8,128)(2,1)S(1)} %shard_map.91) | copy-start | bytes 9437188
  8.0 55.1 %slice-start.1 = ((s8[6258688]{0:T(1024)(128)(4,1)}), s8[2064384]{0:T(1024)(128)(4,1)S(1)}, s32[]{:S(2)}) async-start(s8[6258688]{0:T(1024)(128)(4,1)} %bitcast.8), calls=%async_computation.1 | async-start | bytes 4128768
  8.0 55.2 %copy-start.2 = (f32[512]{0:T(512)S(1)}, f32[512]{0:T(512)}, u32[]{:S(2)}) copy-start(f32[512]{0:T(512)} %param.16) | copy-start | bytes 6148
  63.1 1.6 %copy-start = (bf16[2048,512]{1,0:T(8,128)(2,1)S(1)}, bf16[2048,512]{1,0:T(8,128)(2,1)}, u32[]{:S(2)}) copy-start(bf16[2048,512]{1,0:T(8,128)(2,1)} %wout_ref.1) | copy-start | bytes 6291460
  64.7 1.4 %copy-start.1 = (bf16[768,1024]{1,0:T(8,128)(2,1)S(1)}, bf16[768,1024]{1,0:T(8,128)(2,1)}, u32[]{:S(2)}) copy-start(bf16[768,1024]{1,0:T(8,128)(2,1)} %get-tuple-element.8.aux_ref) | copy-start | bytes 4718596

commit v3 on v2

--- a/solution.py
+++ b/solution.py
@@ -12,7 +12,9 @@
 AUX, COLS, STATE = 1013, 768, 512
 F32, BF16 = jnp.float32, jnp.bfloat16
 VMEM = pltpu.VMEM
-GROUPS, GROUP = 4, 32
+EXCHANGE_VMEM, TAIL_VMEM = 51, 44
+BOUNDS = (0, 56, 88, 112, 128)
+GROUPS = len(BOUNDS) - 1
 TURN = 53
 TURN_BACK = pow(TURN, -1, DEV)
 
@@ -43,7 +45,7 @@
         rows += [-d[i, up], -d[i, 1 - up], -d[i, 2 + up], -d[i, 3 - up]]
     rows += [-d[j, (j - shift) % 4] for shift in range(4)]
     rows += [w[2 * p + up] * w[j] for p in range(2)]
-    return np.broadcast_to(np.stack(rows)[:, :, None], (14, 8, 128)).astype(np.float32).copy()
+    return [[float(v) for v in row] for row in rows]
 
 
 def sublane(shape):
@@ -54,33 +56,26 @@
     return pltpu.roll(x, shift % 8, axis=x.ndim - 2)
 
 
-def pack_kernel(aux_ref, out_ref):
+def pack_tables(pick):
     row = lax.broadcasted_iota(jnp.int32, (512, 384), 0)
     lane = lax.broadcasted_iota(jnp.int32, (512, 384), 1)
     base, slot = row // ROWS * CAP, row % ROWS
-    first = jnp.where((slot < CAP) & (lane == base + slot), 1.0, 0.0).astype(BF16)
-    tail = aux_ref[WIDE:, :].astype(F32)
-    tail = jnp.where(lax.broadcasted_iota(jnp.int32, tail.shape, 0) < AUX - WIDE, tail, 0.0).astype(BF16)
-    nt = (((1,), (1,)), ((), ()))
     for part in range(3):
-        rest = jnp.where((slot >= CAP) & (lane == base + slot - CAP + 4 * part), 1.0, 0.0).astype(BF16)
+        pick[part, :, :384] = jnp.where((slot < CAP) & (lane == base + slot), 1.0, 0.0).astype(BF16)
+        pick[part, :, 384:] = jnp.where((slot >= CAP) & (lane == base + slot - CAP + 4 * part), 1.0, 0.0).astype(BF16)
+
+
+def pack_block(aux, pick, packed, block):
+    lanes = slice(384 * block, 384 * block + 384)
+    last = aux[WIDE:, lanes].astype(F32)
+    last = jnp.concatenate([last, jnp.zeros((WIDE + 256 - AUX, 384), F32)], axis=0).astype(BF16)
+    for part in range(3):
         piece = slice(256 * part, 256 * part + 256)
-        out_ref[:, piece] = (
-            lax.dot_general(first, aux_ref[piece, :], nt, preferred_element_type=F32)
-            + lax.dot_general(rest, tail, nt, preferred_element_type=F32)
-        ).astype(BF16)
-
-
-def pack(aux_t):
-    return pl.pallas_call(
-        pack_kernel,
-        grid=(4,),
-        in_specs=[pl.BlockSpec((1024, 384), lambda g: (0, g))],
-        out_specs=pl.BlockSpec((512, WIDE), lambda g: (g, 0)),
-        out_shape=jax.ShapeDtypeStruct((DEV * ROWS, WIDE), BF16),
-        compiler_params=pltpu.CompilerParams(vmem_limit_bytes=24 << 20),
-        cost_estimate=pl.CostEstimate(flops=3_000_000_000, bytes_accessed=6_500_000, transcendentals=0),
-    )(aux_t)
+        value = lax.dot_general(
+            pick[part], jnp.concatenate([aux[piece, lanes], last], axis=1), (((1,), (1,)), ((), ())),
+            preferred_element_type=F32,
+        )
+        packed[32 * block : 32 * block + 32, :, piece] = value.astype(BF16).reshape(32, ROWS, 256)
 
 
 def section_rows(tab_ref, sec, mass, sums, sides, cells):
@@ -228,18 +223,16 @@
     earlier = jnp.dot(hits.astype(BF16), before, preferred_element_type=F32)
     slot = jnp.sum(hits * earlier, axis=0, keepdims=True)
     base = order.astype(F32) * ROWS
-    none = jnp.full((1, COLS), -1.0, F32)
-    rows = [base + slot]
-    for part in range(3):
-        inside = (slot >= 4 * part) & (slot < 4 * part + 4)
-        rows.append(jnp.where(inside, base + CAP + slot - 4 * part, none))
-    out[...] = jnp.transpose(jnp.concatenate(rows + [none] * 4, axis=0)).astype(jnp.int32)
+    part = (slot >= 4).astype(F32) + (slot >= 8).astype(F32)
+    rows = [base + slot, base + CAP + slot - 4 * part, part]
+    out[...] = jnp.transpose(jnp.concatenate(rows + [part] * 5, axis=0)).astype(jnp.int32)
 
 
 def exchange_kernel(
-    tab_ref, send_ref, owner_ref, bias_ref, prog_ref, mass_ref, win_ref, sec_out, early_out, aux_out,
-    sec, mass, sums, sides, cells, home, win, early, state, acc, places, edge, edge_in, rim, rim_in,
-    load_sem, store_sem, self_sem, send_sem, recv_sem, edge_send, edge_recv, rim_send, rim_recv,
+    owner_hbm, aux_ref, prog_ref, mass_ref, win_ref, sec_out, early_out, aux_out,
+    tab_ref, owner_ref,
+    aux, pick, packed, sec, mass, sums, sides, cells, home, win, early, state, acc, places, edge, edge_in, rim, rim_in,
+    aux_sem, load_sem, store_sem, self_sem, send_sem, recv_sem, edge_send, edge_recv, rim_send, rim_recv,
 ):
     curve, x = lax.axis_index("curve"), lax.axis_index("sub")
     y, z, core = curve // 8, curve // 2 % 4, curve % 2
@@ -250,8 +243,11 @@
         pltpu.make_async_copy(prog_ref, sec, load_sem.at[0]),
         pltpu.make_async_copy(mass_ref, mass, load_sem.at[1]),
         pltpu.make_async_copy(win_ref.at[pl.ds(0, STATE)], win, load_sem.at[2]),
+        pltpu.make_async_copy(owner_hbm, owner_ref, load_sem.at[3]),
     ]
-    for load in loads:
+    slots = [pl.ds(384 * n, 384) for n in range(4)]
+    aux_loads = [pltpu.make_async_copy(aux_ref.at[:, s], aux.at[:, s], aux_sem.at[n]) for n, s in enumerate(slots)]
+    for load in aux_loads + loads:
         load.start()
 
     barrier = pltpu.get_barrier_semaphore()
@@ -262,9 +258,13 @@
         return 0
 
     lax.fori_loop(1, DEV, greet, 0)
+    pack_tables(pick)
+    for n in range(4):
+        aux_loads[n].wait()
+        pack_block(aux, pick, packed, n)
     pl.semaphore_wait(barrier, DEV - 1)
 
-    own = pltpu.make_async_copy(send_ref.at[me], home.at[0], self_sem)
+    own = pltpu.make_async_copy(packed.at[me], home.at[0], self_sem)
     own.start()
 
     def send_group(g):
@@ -275,17 +275,18 @@
                 lax.rem(y + rel // 4 % 4, 4) * 8 + lax.rem(z + rel // 16 % 4, 4) * 2 + lax.rem(core + rel // 64, 2)
             )
             pltpu.make_async_remote_copy(
-                send_ref.at[to_curve * 4 + to_x], home.at[o], send_sem.at[g], recv_sem.at[g],
+                packed.at[to_curve * 4 + to_x], home.at[o], send_sem.at[g], recv_sem.at[g],
                 device_id={"curve": to_curve, "sub": to_x}, device_id_type=mesh,
             ).start()
             return 0
 
-        lax.fori_loop(max(1, GROUP * g), GROUP * g + GROUP, send, 0)
+        lax.fori_loop(max(1, BOUNDS[g]), BOUNDS[g + 1], send, 0)
 
     def group_copy(g):
-        span = pl.ds(max(1, GROUP * g), GROUP - (g == 0))
+        first = max(1, BOUNDS[g])
+        span = pl.ds(first, BOUNDS[g + 1] - first)
         return pltpu.make_async_remote_copy(
-            send_ref.at[span], home.at[span], send_sem.at[g], recv_sem.at[g],
+            packed.at[span], home.at[span], send_sem.at[g], recv_sem.at[g],
             device_id={"curve": curve, "sub": x}, device_id_type=mesh,
         )
 
@@ -294,22 +295,20 @@
         if g == 0:
             own.wait()
 
+        depth = (BOUNDS[g + 1] - BOUNDS[g]) * ROWS
+
         def chunk(m, _):
             rows = pl.ds(m * 256, 256)
-            lane = lax.broadcasted_iota(jnp.int32, (256, GROUP * ROWS), 1) + GROUP * ROWS * g
+            lane = lax.broadcasted_iota(jnp.int32, (256, depth), 1) + BOUNDS[g] * ROWS
 
             def pick(k):
                 return jnp.where(lane == places[rows, k : k + 1], 1.0, 0.0).astype(BF16)
 
-            def block(lanes):
-                return home[GROUP * g : GROUP * (g + 1), :, lanes].reshape(GROUP * ROWS, -1)
-
-            main = jnp.dot(pick(0), block(slice(0, WIDE)), preferred_element_type=F32)
-            rest = jnp.dot(pick(1), block(slice(0, 256)), preferred_element_type=F32)
-            for part in range(1, 3):
-                rest += jnp.dot(
-                    pick(1 + part), block(slice(256 * part, 256 * part + 256)), preferred_element_type=F32
-                )
+            block = home[BOUNDS[g] : BOUNDS[g + 1]].reshape(depth, WIDE)
+            main = jnp.dot(pick(0), block, preferred_element_type=F32)
+            rest = jnp.dot(pick(1), block, preferred_element_type=F32)
+            part = places[rows, 2:3]
+            rest = jnp.where(part == 0, rest[:, :256], jnp.where(part == 1, rest[:, 256:512], rest[:, 512:]))
             if g:
                 main, rest = main + acc[rows, :WIDE], rest + acc[rows, WIDE:]
             if g < GROUPS - 1:
@@ -334,24 +333,30 @@
             copy.wait_recv()
 
     send_group(0)
-    send_group(1)
     loads[0].wait()
     loads[1].wait()
+    sub = sublane((8, LEV))
+    for k, row in enumerate(section_tables()):
+        value = jnp.full((8, LEV), row[0], F32)
+        for n in range(1, 8):
+            value = jnp.where(sub == n, row[n], value)
+        tab_ref[k] = value
     section_rows(tab_ref, sec, mass, sums, sides, cells)
     side_edges(sides, edge)
     edge_copies = both_ways(edge, edge_in, edge_send, edge_recv, "sub", x, 4)
     for copy in edge_copies:
         copy.start()
-    send_group(2)
+    send_group(1)
 
     for f in range(NF):
         state[:, f * LEV : (f + 1) * LEV] = cells[f].astype(BF16)
+    loads[3].wait()
     find_places(owner_ref, (curve, x), places)
     loads[2].wait()
 
     def early_tile(t, _):
         lanes = pl.ds(pl.multiple_of(t * 256, 256), 256)
-        early[:, lanes] = jnp.dot(state[...], win[:, lanes], preferred_element_type=F32) + bias_ref[:, lanes]
+        early[:, lanes] = jnp.dot(state[...], win[:, lanes], preferred_element_type=F32)
         return 0
 
     lax.fori_loop(0, early.shape[1] // 256, early_tile, 0)
@@ -364,6 +369,7 @@
     rim_copies = both_ways(rim, rim_in, rim_send, rim_recv, "curve", curve, 32)
     for copy in rim_copies:
         copy.start()
+    send_group(2)
     send_group(3)
 
     select_group(0)
@@ -382,13 +388,13 @@
     sec_store.wait()
 
 
-def exchange(tab, packed, owner, bias_in, prog, mass, weight_in):
+def exchange(owner, aux_t, prog, mass, weight_in):
     hid = weight_in.shape[1]
     vm, hbm = pl.BlockSpec(memory_space=VMEM), pl.BlockSpec(memory_space=pl.ANY)
     dma = pltpu.SemaphoreType.DMA
     return pl.pallas_call(
         exchange_kernel,
-        in_specs=[vm, vm, vm, vm, hbm, hbm, hbm],
+        in_specs=[hbm] * 5,
         out_specs=[hbm, hbm, vm],
         out_shape=[
             jax.ShapeDtypeStruct(prog.shape, F32),
@@ -396,6 +402,11 @@
             jax.ShapeDtypeStruct((COLS, WIDE + 256), BF16),
         ],
         scratch_shapes=[
+            VMEM((14, 8, LEV), F32),
+            VMEM(owner.shape, jnp.int32),
+            VMEM(aux_t.shape, BF16),
+            VMEM((3, 512, WIDE), BF16),
+            VMEM((DEV, ROWS, WIDE), BF16),
             VMEM(prog.shape, F32),
             VMEM(mass.shape, F32),
             VMEM((NF + 1, EA, EB, 2, 8, LEV), F32),
@@ -411,102 +422,89 @@
             VMEM((2, NF + 1, EA * 4, LEV), BF16),
             VMEM((2, (NF + 1) * 32, LEV), BF16),
             VMEM((2, (NF + 1) * 32, LEV), BF16),
-            dma((3,)), dma((2,)), dma, dma((GROUPS,)), dma((GROUPS,)), dma((2,)), dma((2,)), dma((2,)), dma((2,)),
+            dma((4,)), dma((4,)), dma((2,)), dma, dma((GROUPS,)), dma((GROUPS,)), dma((2,)), dma((2,)), dma((2,)), dma((2,)),
         ],
         compiler_params=pltpu.CompilerParams(
-            collective_id=1, has_side_effects=True, vmem_limit_bytes=56 << 20
+            collective_id=1, has_side_effects=True, vmem_limit_bytes=EXCHANGE_VMEM << 20
         ),
         cost_estimate=pl.CostEstimate(flops=10_000_000_000, bytes_accessed=40_000_000, transcendentals=0),
-    )(tab, packed, owner, bias_in, prog, mass, weight_in)
-
-
-def tail_kernel(
-    aux_ref, early_ref, wa_ref, wb_ref, wout_ref, bout_ref, sec_ref, out_ref, sec, inc, total, load_sem, store_sem
-):
-    step = pl.program_id(0)
-    rows_a = 4
-    pieces = [pl.ds(n * rows_a, rows_a) for n in range(EA // rows_a)]
+    )(owner, aux_t, prog, mass, weight_in)
+
+
+def tail_kernel(aux_ref, early_ref, win_ref, bin_ref, wout_ref, bout_ref, sec_ref, out_ref, inc, spread):
+    step, last = pl.program_id(0), pl.num_programs(0) - 1
+    count = aux_ref.shape[0]
+
+    def add_block():
+        term = jnp.dot(spread[...], inc[...], preferred_element_type=F32)
+        for f in range(NF):
+            piece = term[:, f * LEV : (f + 1) * LEV].reshape(sec_ref.shape[1:])
+            out_ref[f] = sec_ref[f] + piece
+
+    def network_block():
+        total = bout_ref[...]
+        aux = aux_ref[:, :AUX]
+        for n in range(2):
+            lanes = slice(1024 * n, 1024 * n + 1024)
+            h = early_ref[:, lanes] + bin_ref[:, lanes] + jnp.dot(aux, win_ref[STATE:, lanes], preferred_element_type=F32)
+            h = (h / (1.0 + jnp.exp(-h))).astype(BF16)
+            total = total + jnp.dot(h, wout_ref[lanes, :], preferred_element_type=F32)
+        return total.astype(BF16)
+
+    def keep(total):
+        inc[...] = total
 
     @pl.when(step == 0)
     def _():
-        pltpu.make_async_copy(sec_ref, sec, load_sem).start()
-
-    h = (
-        early_ref[...]
-        + jnp.dot(aux_ref[:, :STATE], wa_ref[...], preferred_element_type=F32)
-        + jnp.dot(aux_ref[:, STATE:AUX], wb_ref[: AUX - STATE, :], preferred_element_type=F32)
-    )
-    h = (h / (1.0 + jnp.exp(-h))).astype(BF16)
-    part = jnp.dot(h, wout_ref[...], preferred_element_type=F32)
-
-    @pl.when(step == 0)
+        row = lax.broadcasted_iota(jnp.int32, spread.shape, 0)
+        cell = row // 16 * 4 + row // 8 % 2 * 2 + row % 4 // 2
+        lane = lax.broadcasted_iota(jnp.int32, spread.shape, 1)
+        spread[...] = jnp.where(lane == cell, 1.0, 0.0).astype(BF16)
+        keep(network_block())
+
+    @pl.when((step > 0) & (step < last))
     def _():
-        total[...] = part + bout_ref[...]
-
-    @pl.when(step > 0)
+        add_block()
+        keep(network_block())
+
+    @pl.when(step == last)
     def _():
-        total[...] += part
-
-    @pl.when(step == pl.num_programs(0) - 1)
-    def _():
-        pltpu.make_async_copy(sec_ref, sec, load_sem).wait()
-        right = sublane((8, LEV)) % 4 >= 2
-        stores = []
-        for n, piece in enumerate(pieces):
-            count = rows_a * 32
-            for f in range(NF):
-                inc[f] = total[n * count : (n + 1) * count, f * LEV : (f + 1) * LEV].astype(BF16).astype(F32)
-                for e in range(rows_a * EB):
-                    for p in range(2):
-                        row = e * 4 + 2 * p
-                        term = jnp.where(right, inc[f, row + 1 : row + 2, :], inc[f, row : row + 1, :])
-                        sec[f, n * rows_a + e // EB, e % EB, p] += term
-            store = pltpu.make_async_copy(sec.at[:, piece], out_ref.at[:, piece], store_sem.at[n])
-            store.start()
-            stores.append(store)
-        for store in stores:
-            store.wait()
-
-
-def tail(aux, early, weight_in, weight_out, bias_out, sec):
-    steps = 4
-    hid = early.shape[1]
-    tile = hid // steps
-    hbm = pl.BlockSpec(memory_space=pl.ANY)
+        add_block()
+
+
+def tail(aux, early, weight_in, bias_in, weight_out, bias_out, sec):
+    steps = 3
+    count, rows_a = COLS // steps, EA // steps
+    ahead, behind = lambda n: jnp.minimum(n, steps - 1), lambda n: jnp.maximum(n - 1, 0)
+    whole = pl.BlockSpec(memory_space=VMEM)
+    block = pl.BlockSpec((NF, rows_a, EB, 2, 8, LEV), lambda n: (0, behind(n), 0, 0, 0, 0))
     return pl.pallas_call(
         tail_kernel,
-        grid=(steps,),
+        grid=(steps + 1,),
         in_specs=[
-            pl.BlockSpec(aux.shape, lambda t: (0, 0)),
-            pl.BlockSpec((COLS, tile), lambda t: (0, t)),
-            pl.BlockSpec((STATE, tile), lambda t: (1, t)),
-            pl.BlockSpec((STATE, tile), lambda t: (2, t)),
-            pl.BlockSpec((tile, STATE), lambda t: (t, 0)),
-            pl.BlockSpec((1, STATE), lambda t: (0, 0)),
-            hbm,
+            pl.BlockSpec((count, aux.shape[1]), lambda n: (ahead(n), 0)),
+            pl.BlockSpec((count, early.shape[1]), lambda n: (ahead(n), 0)),
+            whole,
+            whole,
+            whole,
+            whole,
+            block,
         ],
-        out_specs=hbm,
+        out_specs=block,
         out_shape=jax.ShapeDtypeStruct(sec.shape, F32),
-        scratch_shapes=[
-            VMEM(sec.shape, F32),
-            VMEM((NF, 128, LEV), F32),
-            VMEM((COLS, STATE), F32),
-            pltpu.SemaphoreType.DMA,
-            pltpu.SemaphoreType.DMA((EA // 4,)),
-        ],
-        compiler_params=pltpu.CompilerParams(vmem_limit_bytes=40 << 20),
+        scratch_shapes=[VMEM((count, STATE), BF16), VMEM((4 * count, count), BF16)],
+        compiler_params=pltpu.CompilerParams(vmem_limit_bytes=TAIL_VMEM << 20),
         cost_estimate=pl.CostEstimate(flops=5_000_000_000, bytes_accessed=30_000_000, transcendentals=0),
-    )(aux, early, weight_in, weight_in, weight_out, bias_out, sec)
+    )(aux, early, weight_in, bias_in, weight_out, bias_out, sec)
 
 
 def shards(prognostic, layer_mass, column_aux, group_owner, weight_in, bias_in, weight_out, bias_out):
     prog = prognostic.reshape(NF, EA, EB, 2, 8, LEV)
     mass = layer_mass.reshape(EA, EB, 2, 8, LEV)
-    packed = pack(column_aux.T).reshape(DEV, ROWS, WIDE)
     sec, early, aux = exchange(
-        jnp.asarray(section_tables()), packed, group_owner.reshape(1, COLS), bias_in[None], prog, mass, weight_in
+        group_owner.reshape(1, COLS), column_aux.T, prog, mass, weight_in
     )
-    out = tail(aux, early, weight_in, weight_out, bias_out[None], sec)
+    out = tail(aux, early, weight_in, bias_in[None], weight_out, bias_out[None], sec)
     return out.reshape(prognostic.shape)
 
 

time: 79.4 us -> 67.6 us (0.85)
  local copies, waits for them, and re-layouts: 6.55 us -> 0.7 us
  Pallas kernels: 72 us -> 66.7 us
    unnamed x14 -> x10, local copies, waits for them, and re-layouts: 6.55 us -> 0.7 us
    pallas_call x3 -> x2, Pallas kernels: 72 us -> 66.7 us  [the longest x1 54.8 us: exchange(): pl.pallas_call(exchange_kernel, in_specs=[hbm] * 5, out_specs=[hbm, hbm,...]
where the time goes in v3:
time: 67.6 us; the launch traced here: 67.5 us
  Pallas kernels  66.7 us (99%)
  local copies, waits for them, and re-layouts  0.7 us (1%)
    pallas_call x1, Pallas kernels, exchange(): pl.pallas_call(exchange_kernel, in_specs=[hbm] * 5, out_specs=[hbm, hbm,...  54.8 us
    pallas_call x1, Pallas kernels, tail(): pl.pallas_call(tail_kernel, grid=(steps + 1,), in_specs=[pl.BlockSpec((co...  11.9 us

profile of v3, /device:TPU:0, one launch (start us, length us, event | category | flops | bytes accessed | tf_op | source)
XLA Modules:
  0.0 67.5 jit_solution(15698386037521452774)
XLA Ops:
  0.0 0.0 copy-start.4
  0.0 0.7 %copy-done.4 = s32[768,1]{0,1:T(1,128)S(1)} copy-done((s32[768,1]{0,1:T(1,128)S(1)}, s32[768,1]{0,1:T(1,128)}, u32[]{:S(2)}) %copy-start.4) | copy-done | bytes 3096
  0.7 0.0 copy-start
  0.7 0.0 copy-start.1
  0.7 0.0 copy-start.2
  0.7 0.0 copy-start.3
  0.7 54.8 %shard_map.82 = (f32[4,24,8,2,8,128]{5,4,3,2,1,0:T(8,128)}, f32[768,2048]{1,0:T(8,128)}, bf16[768,1024]{1,0:T(8,128)(2,1)S(1)}) custom-call(s32[1,768]{1,0:T(1,128)S(1)} %bitcast.9, bf16[1013,1536]{1,0:T(8,128)(2,1)} %bitcast.11, f32[4,24,8,2,8,128]{5,4,3,2,1,0:T(8,128)} %bitcast.10, f32[24,8,2,8,128]{4,3,2,1,0:T(8,128)} %bitcast.12, bf16[1525,2048]{1,0:T(8,128)(2,1)} %win_ref.3), custom_call_target="tpu_custom_call" | custom-call | flops 10000000000 | bytes 40000000 | tf_op jit(solution)/shard_map/pallas_call | solution.py:395
  55.5 0.0 copy-done
  55.6 0.0 copy-done.1
  55.6 0.0 copy-done.2
  55.6 0.0 copy-done.3
  55.6 11.9 %shard_map.83 = f32[4,24,8,2,8,128]{5,4,3,2,1,0:T(8,128)} custom-call(bf16[768,1024]{1,0:T(8,128)(2,1)S(1)} %get-tuple-element.8.aux_ref, f32[768,2048]{1,0:T(8,128)} %get-tuple-element.9.early_ref, bf16[1525,2048]{1,0:T(8,128)(2,1)S(1)} %copy-done, f32[1,2048]{1,0:T(1,128)S(1)} %bitcast.7, bf16[2048,512]{1,0:T(8,128)(2,1)S(1)} %copy-done.1, ...), custom_call_target="tpu_custom_call" | custom-call | flops 5000000000 | bytes 30000000 | tf_op jit(solution)/shard_map/pallas_call | solution.py:481
Async XLA Ops:
  0.0 0.7 %copy-start.4 = (s32[768,1]{0,1:T(1,128)S(1)}, s32[768,1]{0,1:T(1,128)}, u32[]{:S(2)}) copy-start(s32[768,1]{0,1:T(1,128)} %param.11) | copy-start | bytes 9220
  0.7 54.9 %copy-start = (bf16[1525,2048]{1,0:T(8,128)(2,1)S(1)}, bf16[1525,2048]{1,0:T(8,128)(2,1)}, u32[]{:S(2)}) copy-start(bf16[1525,2048]{1,0:T(8,128)(2,1)} %win_ref.3) | copy-start | bytes 18739204
  0.7 54.9 %copy-start.1 = (bf16[2048,512]{1,0:T(8,128)(2,1)S(1)}, bf16[2048,512]{1,0:T(8,128)(2,1)}, u32[]{:S(2)}) copy-start(bf16[2048,512]{1,0:T(8,128)(2,1)} %wout_ref.1) | copy-start | bytes 6291460
  0.7 54.9 %copy-start.2 = (f32[2048]{0:T(1024)S(1)}, f32[2048]{0:T(1024)}, u32[]{:S(2)}) copy-start(f32[2048]{0:T(1024)} %param.13) | copy-start | bytes 24580
  0.7 54.9 %copy-start.3 = (f32[512]{0:T(512)S(1)}, f32[512]{0:T(512)}, u32[]{:S(2)}) copy-start(f32[512]{0:T(512)} %param.15) | copy-start | bytes 6148

commit v4 on v3

--- a/solution.py
+++ b/solution.py
@@ -8,13 +8,13 @@
 
 section_step = 0.1
 NF, EA, EB, LEV = 4, 24, 8, 128
-DEV, CAP, ROWS, WIDE = 128, 12, 16, 768
+DEV, CAP, ROWS = 128, 12, 16
 AUX, COLS, STATE = 1013, 768, 512
 F32, BF16 = jnp.float32, jnp.bfloat16
 VMEM = pltpu.VMEM
-EXCHANGE_VMEM, TAIL_VMEM = 51, 44
-BOUNDS = (0, 56, 88, 112, 128)
-GROUPS = len(BOUNDS) - 1
+EXCHANGE_VMEM, TAIL_VMEM = 53, 44
+GROUPS = ((0, 0, 64), (0, 64, 128), (1, 0, 64), (1, 64, 104), (1, 104, 128))
+HALF, MAIN, REST = 512, 384, 128
 TURN = 53
 TURN_BACK = pow(TURN, -1, DEV)
 
@@ -67,15 +67,19 @@
 
 def pack_block(aux, pick, packed, block):
     lanes = slice(384 * block, 384 * block + 384)
-    last = aux[WIDE:, lanes].astype(F32)
-    last = jnp.concatenate([last, jnp.zeros((WIDE + 256 - AUX, 384), F32)], axis=0).astype(BF16)
+    last = aux[HALF + MAIN :, lanes].astype(F32)
+    last = jnp.concatenate([last, jnp.zeros((2 * HALF - AUX, 384), F32)], axis=0).astype(BF16)
+    last = jnp.concatenate([aux[MAIN:HALF, lanes], last], axis=0)
     for part in range(3):
-        piece = slice(256 * part, 256 * part + 256)
+        low = 128 * part
+        piece = jnp.concatenate([aux[low : low + 128, lanes], aux[HALF + low : HALF + low + 128, lanes]], axis=0)
         value = lax.dot_general(
-            pick[part], jnp.concatenate([aux[piece, lanes], last], axis=1), (((1,), (1,)), ((), ())),
-            preferred_element_type=F32,
-        )
-        packed[32 * block : 32 * block + 32, :, piece] = value.astype(BF16).reshape(32, ROWS, 256)
+            pick[part], jnp.concatenate([piece, last], axis=1), (((1,), (1,)), ((), ())), preferred_element_type=F32
+        ).astype(BF16)
+        for h in range(2):
+            packed[h, 32 * block : 32 * block + 32, :, low : low + 128] = value[:, 128 * h : 128 * h + 128].reshape(
+                32, ROWS, 128
+            )
 
 
 def section_rows(tab_ref, sec, mass, sums, sides, cells):
@@ -242,7 +246,7 @@
     loads = [
         pltpu.make_async_copy(prog_ref, sec, load_sem.at[0]),
         pltpu.make_async_copy(mass_ref, mass, load_sem.at[1]),
-        pltpu.make_async_copy(win_ref.at[pl.ds(0, STATE)], win, load_sem.at[2]),
+        pltpu.make_async_copy(win_ref.at[pl.ds(0, STATE + HALF)], win, load_sem.at[2]),
         pltpu.make_async_copy(owner_hbm, owner_ref, load_sem.at[3]),
     ]
     slots = [pl.ds(384 * n, 384) for n in range(4)]
@@ -264,10 +268,13 @@
         pack_block(aux, pick, packed, n)
     pl.semaphore_wait(barrier, DEV - 1)
 
-    own = pltpu.make_async_copy(packed.at[me], home.at[0], self_sem)
-    own.start()
+    own = [pltpu.make_async_copy(packed.at[h, me], home.at[h, 0], self_sem.at[h]) for h in range(2)]
+    for copy in own:
+        copy.start()
 
     def send_group(g):
+        h, first, end = GROUPS[g]
+
         def send(o, _):
             rel = lax.rem(o * TURN, DEV)
             to_x = lax.rem(x + rel % 4, 4)
@@ -275,46 +282,48 @@
                 lax.rem(y + rel // 4 % 4, 4) * 8 + lax.rem(z + rel // 16 % 4, 4) * 2 + lax.rem(core + rel // 64, 2)
             )
             pltpu.make_async_remote_copy(
-                packed.at[to_curve * 4 + to_x], home.at[o], send_sem.at[g], recv_sem.at[g],
+                packed.at[h, to_curve * 4 + to_x], home.at[h, o], send_sem.at[g], recv_sem.at[g],
                 device_id={"curve": to_curve, "sub": to_x}, device_id_type=mesh,
             ).start()
             return 0
 
-        lax.fori_loop(max(1, BOUNDS[g]), BOUNDS[g + 1], send, 0)
+        lax.fori_loop(max(1, first), end, send, 0)
 
     def group_copy(g):
-        first = max(1, BOUNDS[g])
-        span = pl.ds(first, BOUNDS[g + 1] - first)
+        h, first, end = GROUPS[g]
+        span = pl.ds(max(1, first), end - max(1, first))
         return pltpu.make_async_remote_copy(
-            packed.at[span], home.at[span], send_sem.at[g], recv_sem.at[g],
+            packed.at[h, span], home.at[h, span], send_sem.at[g], recv_sem.at[g],
             device_id={"curve": curve, "sub": x}, device_id_type=mesh,
         )
 
     def select_group(g):
         group_copy(g).wait_recv()
-        if g == 0:
-            own.wait()
-
-        depth = (BOUNDS[g + 1] - BOUNDS[g]) * ROWS
+        h, first, end = GROUPS[g]
+        if first == 0:
+            own[h].wait()
+        depth = (end - first) * ROWS
 
         def chunk(m, _):
             rows = pl.ds(m * 256, 256)
-            lane = lax.broadcasted_iota(jnp.int32, (256, depth), 1) + BOUNDS[g] * ROWS
+            lane = lax.broadcasted_iota(jnp.int32, (256, depth), 1) + first * ROWS
 
             def pick(k):
                 return jnp.where(lane == places[rows, k : k + 1], 1.0, 0.0).astype(BF16)
 
-            block = home[BOUNDS[g] : BOUNDS[g + 1]].reshape(depth, WIDE)
+            block = home[h, first:end].reshape(depth, MAIN)
             main = jnp.dot(pick(0), block, preferred_element_type=F32)
             rest = jnp.dot(pick(1), block, preferred_element_type=F32)
             part = places[rows, 2:3]
-            rest = jnp.where(part == 0, rest[:, :256], jnp.where(part == 1, rest[:, 256:512], rest[:, 512:]))
-            if g:
-                main, rest = main + acc[rows, :WIDE], rest + acc[rows, WIDE:]
-            if g < GROUPS - 1:
-                acc[rows, :WIDE], acc[rows, WIDE:] = main, rest
+            rest = jnp.where(part == 0, rest[:, :128], jnp.where(part == 1, rest[:, 128:256], rest[:, 256:]))
+            if first:
+                main, rest = main + acc[rows, :MAIN], rest + acc[rows, MAIN:]
+            if end < DEV:
+                acc[rows, :MAIN], acc[rows, MAIN:] = main, rest
+            elif h == 0:
+                state[rows, STATE : STATE + MAIN], state[rows, STATE + MAIN :] = main.astype(BF16), rest.astype(BF16)
             else:
-                aux_out[rows, :WIDE], aux_out[rows, WIDE:] = main.astype(BF16), rest.astype(BF16)
+                aux_out[rows, :MAIN], aux_out[rows, MAIN:] = main.astype(BF16), rest.astype(BF16)
             return 0
 
         lax.fori_loop(0, COLS // 256, chunk, 0)
@@ -333,6 +342,7 @@
             copy.wait_recv()
 
     send_group(0)
+    send_group(1)
     loads[0].wait()
     loads[1].wait()
     sub = sublane((8, LEV))
@@ -346,22 +356,13 @@
     edge_copies = both_ways(edge, edge_in, edge_send, edge_recv, "sub", x, 4)
     for copy in edge_copies:
         copy.start()
-    send_group(1)
+    send_group(2)
 
     for f in range(NF):
         state[:, f * LEV : (f + 1) * LEV] = cells[f].astype(BF16)
     loads[3].wait()
     find_places(owner_ref, (curve, x), places)
-    loads[2].wait()
-
-    def early_tile(t, _):
-        lanes = pl.ds(pl.multiple_of(t * 256, 256), 256)
-        early[:, lanes] = jnp.dot(state[...], win[:, lanes], preferred_element_type=F32)
-        return 0
-
-    lax.fori_loop(0, early.shape[1] // 256, early_tile, 0)
-    early_store = pltpu.make_async_copy(early, early_out, store_sem.at[0])
-    early_store.start()
+    select_group(0)
 
     await_both(edge_copies)
     sides[...] = edge_in[...].astype(F32)
@@ -369,18 +370,27 @@
     rim_copies = both_ways(rim, rim_in, rim_send, rim_recv, "curve", curve, 32)
     for copy in rim_copies:
         copy.start()
-    send_group(2)
     send_group(3)
-
-    select_group(0)
+    send_group(4)
+
     select_group(1)
+    loads[2].wait()
+
+    def early_tile(t, _):
+        lanes = pl.ds(pl.multiple_of(t * 256, 256), 256)
+        early[:, lanes] = jnp.dot(state[...], win[:, lanes], preferred_element_type=F32)
+        return 0
+
+    lax.fori_loop(0, early.shape[1] // 256, early_tile, 0)
+    early_store = pltpu.make_async_copy(early, early_out, store_sem.at[0])
+    early_store.start()
     await_both(rim_copies)
     close_rows(sums, sides, rim_in, sec)
     sec_store = pltpu.make_async_copy(sec, sec_out, store_sem.at[1])
     sec_store.start()
-    select_group(2)
-    select_group(3)
-    for g in range(GROUPS):
+    for g in range(2, len(GROUPS)):
+        select_group(g)
+    for g in range(len(GROUPS)):
         group_copy(g).wait_send()
     for copy in edge_copies + rim_copies:
         copy.wait_send()
@@ -399,30 +409,30 @@
         out_shape=[
             jax.ShapeDtypeStruct(prog.shape, F32),
             jax.ShapeDtypeStruct((COLS, hid), F32),
-            jax.ShapeDtypeStruct((COLS, WIDE + 256), BF16),
+            jax.ShapeDtypeStruct((COLS, HALF), BF16),
         ],
         scratch_shapes=[
             VMEM((14, 8, LEV), F32),
             VMEM(owner.shape, jnp.int32),
             VMEM(aux_t.shape, BF16),
-            VMEM((3, 512, WIDE), BF16),
-            VMEM((DEV, ROWS, WIDE), BF16),
+            VMEM((3, 512, 768), BF16),
+            VMEM((2, DEV, ROWS, MAIN), BF16),
             VMEM(prog.shape, F32),
             VMEM(mass.shape, F32),
             VMEM((NF + 1, EA, EB, 2, 8, LEV), F32),
             VMEM((2, NF + 1, EA * 4, LEV), F32),
             VMEM((NF, COLS, LEV), F32),
-            VMEM((DEV, ROWS, WIDE), BF16),
-            VMEM((STATE, hid), BF16),
+            VMEM((2, DEV, ROWS, MAIN), BF16),
+            VMEM((STATE + HALF, hid), BF16),
             VMEM((COLS, hid), F32),
-            VMEM((COLS, STATE), BF16),
-            VMEM((COLS, WIDE + 256), F32),
+            VMEM((COLS, STATE + HALF), BF16),
+            VMEM((COLS, HALF), F32),
             VMEM((COLS, 8), jnp.int32),
             VMEM((2, NF + 1, EA * 4, LEV), BF16),
             VMEM((2, NF + 1, EA * 4, LEV), BF16),
             VMEM((2, (NF + 1) * 32, LEV), BF16),
             VMEM((2, (NF + 1) * 32, LEV), BF16),
-            dma((4,)), dma((4,)), dma((2,)), dma, dma((GROUPS,)), dma((GROUPS,)), dma((2,)), dma((2,)), dma((2,)), dma((2,)),
+            dma((4,)), dma((4,)), dma((2,)), dma((2,)), dma((len(GROUPS),)), dma((len(GROUPS),)), dma((2,)), dma((2,)), dma((2,)), dma((2,)),
         ],
         compiler_params=pltpu.CompilerParams(
             collective_id=1, has_side_effects=True, vmem_limit_bytes=EXCHANGE_VMEM << 20
@@ -443,10 +453,10 @@
 
     def network_block():
         total = bout_ref[...]
-        aux = aux_ref[:, :AUX]
+        aux = aux_ref[:, : AUX - HALF]
         for n in range(2):
             lanes = slice(1024 * n, 1024 * n + 1024)
-            h = early_ref[:, lanes] + bin_ref[:, lanes] + jnp.dot(aux, win_ref[STATE:, lanes], preferred_element_type=F32)
+            h = early_ref[:, lanes] + bin_ref[:, lanes] + jnp.dot(aux, win_ref[STATE + HALF :, lanes], preferred_element_type=F32)
             h = (h / (1.0 + jnp.exp(-h))).astype(BF16)
             total = total + jnp.dot(h, wout_ref[lanes, :], preferred_element_type=F32)
         return total.astype(BF16)

time: 67.6 us -> 66.6 us (0.985)
  Pallas kernels: 66.7 us -> 65.5 us
    pallas_call x1, Pallas kernels: 11.9 us -> 10.5 us  [tail(): pl.pallas_call(tail_kernel, grid=(steps + 1,), in_specs=[pl.BlockSpec((co...]
where the time goes in v4:
time: 66.6 us; the launch traced here: 66.3 us
  Pallas kernels  65.5 us (98%)
  local copies, waits for them, and re-layouts  0.7 us (1%)
    pallas_call x1, Pallas kernels, exchange(): pl.pallas_call(exchange_kernel, in_specs=[hbm] * 5, out_specs=[hbm, hbm,...  55 us
    pallas_call x1, Pallas kernels, tail(): pl.pallas_call(tail_kernel, grid=(steps + 1,), in_specs=[pl.BlockSpec((co...  10.5 us

profile of v4, /device:TPU:0, one launch (start us, length us, event | category | flops | bytes accessed | tf_op | source)
XLA Modules:
  0.0 66.3 jit_solution(7522061726395505383)
XLA Ops:
  0.0 0.0 copy-start.4
  0.0 0.7 %copy-done.4 = s32[768,1]{0,1:T(1,128)S(1)} copy-done((s32[768,1]{0,1:T(1,128)S(1)}, s32[768,1]{0,1:T(1,128)}, u32[]{:S(2)}) %copy-start.4) | copy-done | bytes 3096
  0.7 0.0 copy-start
  0.7 0.0 copy-start.1
  0.7 0.0 copy-start.2
  0.7 0.0 copy-start.3
  0.7 55.0 %shard_map.82 = (f32[4,24,8,2,8,128]{5,4,3,2,1,0:T(8,128)}, f32[768,2048]{1,0:T(8,128)}, bf16[768,512]{1,0:T(8,128)(2,1)S(1)}) custom-call(s32[1,768]{1,0:T(1,128)S(1)} %bitcast.9, bf16[1013,1536]{1,0:T(8,128)(2,1)} %bitcast.11, f32[4,24,8,2,8,128]{5,4,3,2,1,0:T(8,128)} %bitcast.10, f32[24,8,2,8,128]{4,3,2,1,0:T(8,128)} %bitcast.12, bf16[1525,2048]{1,0:T(8,128)(2,1)} %win_ref.3), custom_call_target="tpu_custom_call" | custom-call | flops 10000000000 | bytes 40000000 | tf_op jit(solution)/shard_map/pallas_call | solution.py:405
  55.7 0.0 copy-done
  55.7 0.0 copy-done.1
  55.7 0.0 copy-done.2
  55.7 0.0 copy-done.3
  55.8 10.5 %shard_map.83 = f32[4,24,8,2,8,128]{5,4,3,2,1,0:T(8,128)} custom-call(bf16[768,512]{1,0:T(8,128)(2,1)S(1)} %get-tuple-element.8.aux_ref, f32[768,2048]{1,0:T(8,128)} %get-tuple-element.9.early_ref, bf16[1525,2048]{1,0:T(8,128)(2,1)S(1)} %copy-done, f32[1,2048]{1,0:T(1,128)S(1)} %bitcast.7, bf16[2048,512]{1,0:T(8,128)(2,1)S(1)} %copy-done.1, ...), custom_call_target="tpu_custom_call" | custom-call | flops 5000000000 | bytes 30000000 | tf_op jit(solution)/shard_map/pallas_call | solution.py:491
Async XLA Ops:
  0.0 0.7 %copy-start.4 = (s32[768,1]{0,1:T(1,128)S(1)}, s32[768,1]{0,1:T(1,128)}, u32[]{:S(2)}) copy-start(s32[768,1]{0,1:T(1,128)} %param.11) | copy-start | bytes 9220
  0.7 55.0 %copy-start = (bf16[1525,2048]{1,0:T(8,128)(2,1)S(1)}, bf16[1525,2048]{1,0:T(8,128)(2,1)}, u32[]{:S(2)}) copy-start(bf16[1525,2048]{1,0:T(8,128)(2,1)} %win_ref.3) | copy-start | bytes 18739204
  0.7 55.0 %copy-start.1 = (bf16[2048,512]{1,0:T(8,128)(2,1)S(1)}, bf16[2048,512]{1,0:T(8,128)(2,1)}, u32[]{:S(2)}) copy-start(bf16[2048,512]{1,0:T(8,128)(2,1)} %wout_ref.1) | copy-start | bytes 6291460
  0.7 55.0 %copy-start.2 = (f32[2048]{0:T(1024)S(1)}, f32[2048]{0:T(1024)}, u32[]{:S(2)}) copy-start(f32[2048]{0:T(1024)} %param.13) | copy-start | bytes 24580
  0.7 55.1 %copy-start.3 = (f32[512]{0:T(512)S(1)}, f32[512]{0:T(512)}, u32[]{:S(2)}) copy-start(f32[512]{0:T(512)} %param.15) | copy-start | bytes 6148

commit v5 on v4

--- a/solution.py
+++ b/solution.py
@@ -13,7 +13,7 @@
 F32, BF16 = jnp.float32, jnp.bfloat16
 VMEM = pltpu.VMEM
 EXCHANGE_VMEM, TAIL_VMEM = 53, 44
-GROUPS = ((0, 0, 64), (0, 64, 128), (1, 0, 64), (1, 64, 104), (1, 104, 128))
+GROUPS = ((0, 0, 64), (0, 64, 128), (1, 0, 64), (1, 64, 112), (1, 112, 128))
 HALF, MAIN, REST = 512, 384, 128
 TURN = 53
 TURN_BACK = pow(TURN, -1, DEV)
@@ -454,8 +454,8 @@
     def network_block():
         total = bout_ref[...]
         aux = aux_ref[:, : AUX - HALF]
-        for n in range(2):
-            lanes = slice(1024 * n, 1024 * n + 1024)
+        for n in range(1):
+            lanes = slice(2048 * n, 2048 * n + 2048)
             h = early_ref[:, lanes] + bin_ref[:, lanes] + jnp.dot(aux, win_ref[STATE + HALF :, lanes], preferred_element_type=F32)
             h = (h / (1.0 + jnp.exp(-h))).astype(BF16)
             total = total + jnp.dot(h, wout_ref[lanes, :], preferred_element_type=F32)

time: 66.6 us -> 66.3 us (level)
  no operation moved by 1% of the time
where the time goes in v5:
time: 66.3 us; the launch traced here: 65.8 us
  Pallas kernels  65.1 us (98%)
  local copies, waits for them, and re-layouts  0.7 us (1%)
    pallas_call x1, Pallas kernels, exchange(): pl.pallas_call(exchange_kernel, in_specs=[hbm] * 5, out_specs=[hbm, hbm,...  54.7 us
    pallas_call x1, Pallas kernels, tail(): pl.pallas_call(tail_kernel, grid=(steps + 1,), in_specs=[pl.BlockSpec((co...  10.4 us

profile of v5, /device:TPU:0, one launch (start us, length us, event | category | flops | bytes accessed | tf_op | source)
XLA Modules:
  0.0 65.8 jit_solution(4007280134663183457)
XLA Ops:
  0.0 0.0 copy-start.4
  0.0 0.7 %copy-done.4 = s32[768,1]{0,1:T(1,128)S(1)} copy-done((s32[768,1]{0,1:T(1,128)S(1)}, s32[768,1]{0,1:T(1,128)}, u32[]{:S(2)}) %copy-start.4) | copy-done | bytes 3096
  0.7 0.0 copy-start
  0.7 0.0 copy-start.1
  0.7 0.0 copy-start.2
  0.7 0.0 copy-start.3
  0.7 54.7 %shard_map.82 = (f32[4,24,8,2,8,128]{5,4,3,2,1,0:T(8,128)}, f32[768,2048]{1,0:T(8,128)}, bf16[768,512]{1,0:T(8,128)(2,1)S(1)}) custom-call(s32[1,768]{1,0:T(1,128)S(1)} %bitcast.9, bf16[1013,1536]{1,0:T(8,128)(2,1)} %bitcast.11, f32[4,24,8,2,8,128]{5,4,3,2,1,0:T(8,128)} %bitcast.10, f32[24,8,2,8,128]{4,3,2,1,0:T(8,128)} %bitcast.12, bf16[1525,2048]{1,0:T(8,128)(2,1)} %win_ref.3), custom_call_target="tpu_custom_call" | custom-call | flops 10000000000 | bytes 40000000 | tf_op jit(solution)/shard_map/pallas_call | solution.py:405
  55.4 0.0 copy-done
  55.4 0.0 copy-done.1
  55.4 0.0 copy-done.2
  55.4 0.0 copy-done.3
  55.4 10.4 %shard_map.83 = f32[4,24,8,2,8,128]{5,4,3,2,1,0:T(8,128)} custom-call(bf16[768,512]{1,0:T(8,128)(2,1)S(1)} %get-tuple-element.8.aux_ref, f32[768,2048]{1,0:T(8,128)} %get-tuple-element.9.early_ref, bf16[1525,2048]{1,0:T(8,128)(2,1)S(1)} %copy-done, f32[1,2048]{1,0:T(1,128)S(1)} %bitcast.7, bf16[2048,512]{1,0:T(8,128)(2,1)S(1)} %copy-done.1, ...), custom_call_target="tpu_custom_call" | custom-call | flops 5000000000 | bytes 30000000 | tf_op jit(solution)/shard_map/pallas_call | solution.py:491
Async XLA Ops:
  0.0 0.7 %copy-start.4 = (s32[768,1]{0,1:T(1,128)S(1)}, s32[768,1]{0,1:T(1,128)}, u32[]{:S(2)}) copy-start(s32[768,1]{0,1:T(1,128)} %param.11) | copy-start | bytes 9220
  0.7 54.7 %copy-start = (bf16[1525,2048]{1,0:T(8,128)(2,1)S(1)}, bf16[1525,2048]{1,0:T(8,128)(2,1)}, u32[]{:S(2)}) copy-start(bf16[1525,2048]{1,0:T(8,128)(2,1)} %win_ref.3) | copy-start | bytes 18739204
  0.7 54.7 %copy-start.1 = (bf16[2048,512]{1,0:T(8,128)(2,1)S(1)}, bf16[2048,512]{1,0:T(8,128)(2,1)}, u32[]{:S(2)}) copy-start(bf16[2048,512]{1,0:T(8,128)(2,1)} %wout_ref.1) | copy-start | bytes 6291460
  0.7 54.7 %copy-start.2 = (f32[2048]{0:T(1024)S(1)}, f32[2048]{0:T(1024)}, u32[]{:S(2)}) copy-start(f32[2048]{0:T(1024)} %param.13) | copy-start | bytes 24580
  0.7 54.7 %copy-start.3 = (f32[512]{0:T(512)S(1)}, f32[512]{0:T(512)}, u32[]{:S(2)}) copy-start(f32[512]{0:T(512)} %param.15) | copy-start | bytes 6148
